TPU v7x, 512 devices: a whole 4x8x8 slice. The times are simulated.
512 devices in a mesh: seq: 64 (over z, x, core), head: 8 (over y).
Axes of the slice: x: 4, y: 8, z: 8, core: 2. Of those that a mesh axis runs over, the one named last changes fastest.
Arguments:
- head_inputs: bfloat16 [65536, 5120], P(('seq', 'head')), may hold values from -6 to 6
- step_sizes: bfloat16 [65536, 80], P(('seq', 'head')), may hold values from 0.05 to 2
- decay_rates: bfloat16 [65536, 80], P(('seq', 'head')), may hold values from 0 to 1
- input_map: bfloat16 [65536, 128], P(('seq', 'head')), may hold values from -0.47851562 to 0.47851562
- output_map: bfloat16 [65536, 128], P(('seq', 'head')), may hold values from -0.47851562 to 0.47851562
- skip_gain: float32 [80], replicated, may hold values from 0.5 to 1.5
Outputs:
- mixed_heads: bfloat16 [65536, 5120], P(('seq', 'head'))
All inputs are finite; a program needn't handle non-finite values.
Results may differ from a plain program's by a relative error of at most 0.009.
Values may be sent and summed in bfloat16 or wider, within the bound.
No kernel may reach another device: no remote copies, remote signals or barrier semaphores. Data moves between devices by JAX's collectives and lax.ppermute only.
A program may use at most 128 MiB of HBM per device.

v0:
```python
import jax
import jax.numpy as jnp
from jax import lax
from jax.sharding import PartitionSpec as P

STRETCH = 256


highest = lax.Precision.HIGHEST


def entering(value, axis, join, neutral):
    count, mine = (lax.axis_size(axis), lax.axis_index(axis))
    pieces = jax.tree.map(lambda part: lax.all_gather(part, axis), value)
    total = jax.tree.map(
        lambda part, zero: jnp.full_like(part, 0) + jnp.asarray(zero, part.dtype), value, neutral
    )

    def lap(position, total):
        longer = join(total, jax.tree.map(lambda part: part[position], pieces))
        return jax.tree.map(lambda new, old: jnp.where(position < mine, new, old), longer, total)

    return lax.fori_loop(0, count - 1, lap, total)


def ssd_block(carry_state, offset, values, step_vals, rate_vals, in_rows, out_rows, skip_part):
    length = rate_vals.shape[0]
    cumulative = jnp.cumsum(rate_vals, axis=0)
    later_pos = lax.broadcasted_iota(jnp.int32, (length, length), 0)
    earlier_pos = lax.broadcasted_iota(jnp.int32, (length, length), 1)
    causal = (later_pos >= earlier_pos)[:, :, None]
    decay_spans = cumulative[:, None, :] - cumulative[None, :, :]
    weights = jnp.where(causal, jnp.exp(-jnp.where(causal, decay_spans, 0.0)), 0.0)
    intersections = jnp.dot(out_rows, in_rows.T, precision=highest)
    scaled = step_vals[:, :, None] * values
    inner_part = jnp.einsum(
        "tsh,shp->thp", weights * intersections[:, :, None], scaled, precision=highest
    )
    carried = jnp.exp(-cumulative)[:, :, None] * jnp.einsum(
        "tn,hpn->thp", out_rows, carry_state, precision=highest
    )
    result = inner_part + carried + skip_part[None, :, None] * values
    block_sum = cumulative[-1]
    tail_weights = jnp.exp(cumulative - block_sum[None, :])
    new_state = jnp.exp(-block_sum)[:, None, None] * carry_state + jnp.einsum(
        "shp,sn->hpn", tail_weights[:, :, None] * scaled, in_rows, precision=highest
    )
    return (new_state, offset + block_sum, result, offset[None, :] + cumulative)


def chain_link(earlier, following):
    return (earlier[0] * following[0], following[0][:, None, None] * earlier[1] + following[1])


def local(head_inputs, step_sizes, decay_rates, input_map, output_map, skip_gain):
    groups = lax.axis_size("head")
    head_count = step_sizes.shape[1]
    head_dim = head_inputs.shape[1] // head_count
    heads_dev = head_count // groups
    block_inputs, block_steps, block_rates = (
        lax.all_to_all(head_inputs, "head", split_axis=1, concat_axis=0, tiled=True),
        lax.all_to_all(step_sizes, "head", split_axis=1, concat_axis=0, tiled=True),
        lax.all_to_all(decay_rates, "head", split_axis=1, concat_axis=0, tiled=True),
    )
    block_in, block_out = (
        lax.all_gather(input_map, "head", axis=0, tiled=True),
        lax.all_gather(output_map, "head", axis=0, tiled=True),
    )
    skip_part = lax.dynamic_slice_in_dim(skip_gain, lax.axis_index("head") * heads_dev, heads_dev)
    block_len = block_inputs.shape[0]
    stretch_count = block_len // STRETCH
    state_dim = block_in.shape[1]
    out_rows_all = block_out.astype(jnp.float32)
    pieces = (
        block_inputs.astype(jnp.float32).reshape(stretch_count, STRETCH, heads_dev, head_dim),
        block_steps.astype(jnp.float32).reshape(stretch_count, STRETCH, heads_dev),
        block_rates.astype(jnp.float32).reshape(stretch_count, STRETCH, heads_dev),
        block_in.astype(jnp.float32).reshape(stretch_count, STRETCH, state_dim),
        out_rows_all.reshape(stretch_count, STRETCH, state_dim),
    )

    def advance(running, piece):
        new_state, new_offset, result, cumulative = ssd_block(
            running[0], running[1], piece[0], piece[1], piece[2], piece[3], piece[4], skip_part
        )
        return ((new_state, new_offset), (result, cumulative))

    start_state = jnp.zeros((heads_dev, head_dim, state_dim), jnp.float32)
    start_offset = jnp.zeros((heads_dev,), jnp.float32)
    (block_state, block_sum), (local_out, cumulative) = lax.scan(
        advance, (start_state, start_offset), pieces
    )
    local_out = local_out.reshape(block_len, heads_dev, head_dim)
    cumulative = cumulative.reshape(block_len, heads_dev)
    entering_decay, entering_state = entering(
        (jnp.exp(-block_sum), block_state),
        "seq",
        chain_link,
        (jnp.ones_like(block_sum), jnp.zeros_like(block_state)),
    )
    correction = jnp.exp(-cumulative)[:, :, None] * jnp.einsum(
        "tn,hpn->thp", out_rows_all, entering_state, precision=highest
    )
    finished = (
        (local_out + correction).reshape(block_len, heads_dev * head_dim).astype(jnp.bfloat16)
    )
    return lax.all_to_all(finished, "head", split_axis=0, concat_axis=1, tiled=True)


def solution(mesh):
    placed = (
        P(("seq", "head"), None),
        P(("seq", "head"), None),
        P(("seq", "head"), None),
        P(("seq", "head"), None),
        P(("seq", "head"), None),
        P(),
    )
    return jax.shard_map(
        local, mesh=mesh, in_specs=placed, out_specs=P(("seq", "head"), None), check_vma=False
    )
```

profile of v0, /device:TPU:1, one launch (start us, length us, event | category | flops | bytes accessed | tf_op | source)
XLA Modules:
  0.0 485.1 jit_solution(4316728587847442559)
XLA Ops:
  7.9 7.7 %all-to-all-start = ((bf16[128,8,10]{0,2,1:T(8,128)(2,1)}), bf16[128,8,10]{0,2,1:T(8,128)(2,1)S(1)}, u32[]{:S(2)}, u32[]{:S(2)}) async-start(bf16[128,8,10]{0,2,1:T(8,128)(2,1)} %all_to_all.42), calls=%async_computation | async-start | bytes 65536 | tf_op jit(solution)/shard_map/all_to_all | solution.py:63
  16.9 5.6 %all-to-all-done = bf16[128,8,10]{0,2,1:T(8,128)(2,1)S(1)} async-done(((bf16[128,8,10]{0,2,1:T(8,128)(2,1)}), bf16[128,8,10]{0,2,1:T(8,128)(2,1)S(1)}, u32[]{:S(2)}, u32[]{:S(2)}) %all-to-all-start) | async-done | bytes 20512 | tf_op jit(solution)/shard_map/all_to_all | solution.py:63
  22.5 3.3 all-to-all-start.1
  25.9 2.4 copy.38
  28.3 4.3 all-to-all-done.1
  32.6 3.6 all-to-all-start.2
  36.3 43.4 %all_gather.19 = bf16[1024,128]{1,0:T(8,128)(2,1)S(1)} all-gather(bf16[128,128]{1,0:T(8,128)(2,1)S(1)} %copy-done.4), channel_id=1, replica_groups=mesh['seq'=64,'head'=8] {'head'}, dimensions={0}, use_global_device_ids=true | all-gather | bytes 294912 | tf_op jit(solution)/shard_map/all_gather | solution.py:67
  80.6 19.2 %all_gather.18 = bf16[1024,128]{1,0:T(8,128)(2,1)S(1)} all-gather(bf16[128,128]{1,0:T(8,128)(2,1)S(1)} %copy-done.5), channel_id=1, replica_groups=mesh['seq'=64,'head'=8] {'head'}, dimensions={0}, use_global_device_ids=true | all-gather | bytes 294912 | tf_op jit(solution)/shard_map/all_gather | solution.py:66
  100.9 1.5 copy.39
  102.4 2.3 reshape.92
  104.7 108.2 %while.31 = (s32[]{:T(128)}, f32[10,64,128]{2,1,0:T(8,128)S(1)}, f32[10]{0:T(128)}, f32[4,256,10,64]{1,0,3,2:T(4,128)}, f32[4,256,10]{1,2,0:T(8,128)}, /*index=5...) while((s32[]{:T(128)}, f32[10,64,128]{2,1,0:T(8,128)S(1)}, ...), condition=%wide.region_3.4_spmd.clone, body=%wide.region_0.3_spmd.clone.sunk | while | flops 1112448512 | bytes 10395849 | solution.py:90
  107.0 2.4 constant_dynamic-slice_fusion.5
  109.5 3.1 fusion.70
  112.9 1.6 fusion.71
  115.2 15.1 %dynamic_update_slice.14 = f32[4,256,10,64]{1,0,3,2:T(4,128)} dynamic-update-slice(f32[4,256,10,64]{1,0,3,2:T(4,128)} %get-tuple-element.419, f32[1,256,10,64]{1,0,3,2:T(1,128)S(1)} %copy.87, s32[]{:T(128)} %get-tuple-element.416, s32[]{:T(128)} %constant.57.clone.1..sunk, s32[]{:T(128)} %constant.57.clone.1..sunk, s32[]{:T(128)} %constant.57.clone.1..sunk) | dynamic-update-slice | bytes 1310724 | tf_op jit(solution)/shard_map/while/body/jit(dynamic_update_index_in_dim)/dynamic_update_slice | solution.py:90
  134.1 2.4 constant_dynamic-slice_fusion.5
  136.5 3.1 fusion.70
  139.9 1.6 fusion.71
  142.2 15.1 %dynamic_update_slice.14 = f32[4,256,10,64]{1,0,3,2:T(4,128)} dynamic-update-slice(f32[4,256,10,64]{1,0,3,2:T(4,128)} %get-tuple-element.419, f32[1,256,10,64]{1,0,3,2:T(1,128)S(1)} %copy.87, s32[]{:T(128)} %get-tuple-element.416, s32[]{:T(128)} %constant.57.clone.1..sunk, s32[]{:T(128)} %constant.57.clone.1..sunk, s32[]{:T(128)} %constant.57.clone.1..sunk) | dynamic-update-slice | bytes 1310724 | tf_op jit(solution)/shard_map/while/body/jit(dynamic_update_index_in_dim)/dynamic_update_slice | solution.py:90
  161.1 2.4 constant_dynamic-slice_fusion.5
  163.6 3.1 fusion.70
  167.0 1.6 fusion.71
  169.3 15.1 %dynamic_update_slice.14 = f32[4,256,10,64]{1,0,3,2:T(4,128)} dynamic-update-slice(f32[4,256,10,64]{1,0,3,2:T(4,128)} %get-tuple-element.419, f32[1,256,10,64]{1,0,3,2:T(1,128)S(1)} %copy.87, s32[]{:T(128)} %get-tuple-element.416, s32[]{:T(128)} %constant.57.clone.1..sunk, s32[]{:T(128)} %constant.57.clone.1..sunk, s32[]{:T(128)} %constant.57.clone.1..sunk) | dynamic-update-slice | bytes 1310724 | tf_op jit(solution)/shard_map/while/body/jit(dynamic_update_index_in_dim)/dynamic_update_slice | solution.py:90
  188.1 2.4 constant_dynamic-slice_fusion.5
  190.6 3.1 fusion.70
  194.0 1.6 fusion.71
  196.3 15.1 %dynamic_update_slice.14 = f32[4,256,10,64]{1,0,3,2:T(4,128)} dynamic-update-slice(f32[4,256,10,64]{1,0,3,2:T(4,128)} %get-tuple-element.419, f32[1,256,10,64]{1,0,3,2:T(1,128)S(1)} %copy.87, s32[]{:T(128)} %get-tuple-element.416, s32[]{:T(128)} %constant.57.clone.1..sunk, s32[]{:T(128)} %constant.57.clone.1..sunk, s32[]{:T(128)} %constant.57.clone.1..sunk) | dynamic-update-slice | bytes 1310724 | tf_op jit(solution)/shard_map/while/body/jit(dynamic_update_index_in_dim)/dynamic_update_slice | solution.py:90
  216.5 144.4 %all-reduce = f32[640]{0:T(1024)S(1)} all-reduce(f32[640]{0:T(1024)S(1)} %exponential_dynamic-update-slice_fusion), channel_id=2, replica_groups=mesh['seq'=64,'head'=8] {'seq'}, use_global_device_ids=true, to_apply=%add | all-reduce | flops 640 | bytes 5120
  361.0 3.2 reshape.89
  364.4 70.8 %while.32 = (s32[]{:T(128)}, f32[10,64,128]{2,1,0:T(8,128)S(1)}, s32[]{:T(128)}, f32[64,10]{1,0:T(8,128)S(1)}, f32[64,10,64,128]{3,2,1,0:T(8,128)}, /*index=5*/s32[]{:T(128)}, s32[]{:T(128)}) while((s32[]{:T(128)}, f32[10,64,128]{2,1,0:T(8,128)S(1)}, s32[]{:T(128)}, f32[64,10]{1,0:T(8,128)S(1)}, f32[64,10,64,128]{3,2,1,0:T(8,128)}, ...), condition=%wide.region_5.6_spmd.clone, body=%wide.region_4.5_spmd.clone.sunk | while | flops 327684 | bytes 983265 | solution.py:23
  437.0 39.9 %all_to_all.55 = bf16[8,128,640]{1,2,0:T(8,128)(2,1)S(1)} all-to-all(bf16[8,128,640]{1,2,0:T(8,128)(2,1)S(1)} %copy.45), channel_id=1, replica_groups=mesh['seq'=64,'head'=8] {'head'}, dimensions={0} | all-to-all | bytes 2621440 | tf_op jit(solution)/shard_map/all_to_all | solution.py:107
  476.9 1.4 copy.46
  (280 shorter events, 96.9 us)
Async XLA Ops:
  7.9 14.6 %all-to-all-start = ((bf16[128,8,10]{0,2,1:T(8,128)(2,1)}), bf16[128,8,10]{0,2,1:T(8,128)(2,1)S(1)}, u32[]{:S(2)}, u32[]{:S(2)}) async-start(bf16[128,8,10]{0,2,1:T(8,128)(2,1)} %all_to_all.42), calls=%async_computation | async-start | bytes 65536 | tf_op jit(solution)/shard_map/all_to_all | solution.py:63
  22.5 10.1 %all-to-all-start.1 = ((bf16[128,8,10]{0,2,1:T(8,128)(2,1)}), bf16[128,8,10]{0,2,1:T(8,128)(2,1)S(1)}, u32[]{:S(2)}, u32[]{:S(2)}) async-start(bf16[128,8,10]{0,2,1:T(8,128)(2,1)} %all_to_all.44), calls=%async_computation.1 | async-start | bytes 65536 | tf_op jit(solution)/shard_map/all_to_all | solution.py:62
  25.8 10.5 %copy-start.4 = (bf16[128,128]{1,0:T(8,128)(2,1)S(1)}, bf16[128,128]{1,0:T(8,128)(2,1)}, u32[]{:S(2)}) copy-start(bf16[128,128]{1,0:T(8,128)(2,1)} %param.14) | copy-start | bytes 98308
  25.9 54.8 %copy-start.5 = (bf16[128,128]{1,0:T(8,128)(2,1)S(1)}, bf16[128,128]{1,0:T(8,128)(2,1)}, u32[]{:S(2)}) copy-start(bf16[128,128]{1,0:T(8,128)(2,1)} %param.13) | copy-start | bytes 98308
  28.3 71.6 %copy-start.9 = (f32[80]{0:T(128)S(1)}, f32[80]{0:T(128)}, u32[]{:S(2)}) copy-start(f32[80]{0:T(128)} %param.15) | copy-start | bytes 964
  32.6 68.1 %all-to-all-start.2 = ((bf16[128,8,640]{0,2,1:T(8,128)(2,1)}), bf16[128,8,640]{0,2,1:T(8,128)(2,1)S(1)}, u32[]{:S(2)}, u32[]{:S(2)}) async-start(bf16[128,8,640]{0,2,1:T(8,128)(2,1)} %bitcast.2), calls=%async_computation.2 | async-start | bytes 2621440 | tf_op jit(solution)/shard_map/all_to_all | solution.py:61
  36.2 328.1 %all-gather.4.cloned.1.call-start = ((), (), s32[]{:S(2)}) async-start(), calls=%async_computation.4 | async-start | bytes 21299200 | tf_op jit(solution)/shard_map/all_gather | solution.py:14
  79.8 20.1 %copy-start.1 = (bf16[1024,128]{1,0:T(8,128)(2,1)}, bf16[1024,128]{1,0:T(8,128)(2,1)S(1)}, u32[]{:S(2)}) copy-start(bf16[1024,128]{1,0:T(8,128)(2,1)S(1)} %all_gather.19) | copy-start | bytes 786436
  109.5 3.4 copy-start.6
  112.6 17.7 %copy-start.7 = (f32[10]{0:T(128)S(1)}, f32[10]{0:T(128)}, u32[]{:S(2)}) copy-start(f32[10]{0:T(128)} %get-tuple-element.418) | copy-start | bytes 124 | tf_op jit(solution)/shard_map/while
  130.3 1.5 copy-start.8
  136.5 3.4 copy-start.6
  139.6 17.7 %copy-start.7 = (f32[10]{0:T(128)S(1)}, f32[10]{0:T(128)}, u32[]{:S(2)}) copy-start(f32[10]{0:T(128)} %get-tuple-element.418) | copy-start | bytes 124 | tf_op jit(solution)/shard_map/while
  157.3 1.5 copy-start.8
  163.6 3.4 copy-start.6
  166.7 17.7 %copy-start.7 = (f32[10]{0:T(128)S(1)}, f32[10]{0:T(128)}, u32[]{:S(2)}) copy-start(f32[10]{0:T(128)} %get-tuple-element.418) | copy-start | bytes 124 | tf_op jit(solution)/shard_map/while
  184.4 1.5 copy-start.8
  190.6 3.4 copy-start.6
  193.7 17.7 %copy-start.7 = (f32[10]{0:T(128)S(1)}, f32[10]{0:T(128)}, u32[]{:S(2)}) copy-start(f32[10]{0:T(128)} %get-tuple-element.418) | copy-start | bytes 124 | tf_op jit(solution)/shard_map/while
  211.4 1.5 copy-start.8
  212.9 0.7 copy-start
  361.0 3.2 copy-start.3
  364.3 70.8 %copy-start.2 = (bf16[1024,128]{1,0:T(8,128)(2,1)S(1)}, bf16[1024,128]{1,0:T(8,128)(2,1)}, u32[]{:S(2)}) copy-start(bf16[1024,128]{1,0:T(8,128)(2,1)} %copy-done.1) | copy-start | bytes 786436
Sparse Core Ops, SparseCore 0:
  213.8 133.4 all-gather.3
where the time goes:
time: 490 us; the launch traced here: 485 us
  blocking collectives  247 us (50%)
  local copies, waits for them, and re-layouts  92.1 us (19%)
  other arithmetic  76 us (16%)
  matrix products  28.6 us (6%)
  starting transfers between devices  14.6 us (3%)
  between operations  14.4 us (3%)
  waiting for transfers between devices  10 us (2%)
    unnamed x1, blocking collectives  144 us
    select_n x63, other arithmetic, lap(): jnp.where(position < mine, new, old)  68.2 us
    dynamic_update_slice x8, local copies, waits for them, and re-layouts, local(): lax.scan(advance, (start_state, start_offset), pieces)  63 us
    all_gather x1, blocking collectives, local(): lax.all_gather(output_map, 'head', axis=0, tiled=True)  43.4 us
    all_to_all x1, blocking collectives, local(): lax.all_to_all(finished, 'head', split_axis=0, concat_axis=1, tiled=True)  39.9 us
    all_gather x1, blocking collectives, local(): lax.all_gather(input_map, 'head', axis=0, tiled=True)  19.2 us
    dot_general x4, matrix products, ssd_block(): jnp.einsum('tsh,shp->thp', weights * intersections[:, :, None], scaled, p...  12.4 us
    dynamic_slice x16, local copies, waits for them, and re-layouts, local(): lax.scan(advance, (start_state, start_offset), pieces)  9.83 us
  transfers between devices with their start and end apart: 4, of which 2 were waited for; matrix products, arithmetic and copies ran while one was open for 2% of the time, Pallas kernels for 0%

commit v1 on v0

v1 whole, which is shorter than its diff:
```python
import functools

import jax
import jax.numpy as jnp
from jax import lax
from jax.experimental import pallas as pl
from jax.experimental.pallas import tpu as pltpu
from jax.sharding import Mesh
from jax.sharding import PartitionSpec as P

HEADS = 80
HEAD_DIM = 64
STATE = 128
TOK = 128
HB = 10
COLS = HB * HEAD_DIM
NB = HEADS // HB
NA = 8
ROWS = STATE // NA
TILES = COLS // 128
DEC = 8
PARTS = ((0, 5),)
STEPS = 4
BPS = NB // STEPS

f32, bf16 = jnp.float32, jnp.bfloat16


def iota(shape, dim):
    return lax.broadcasted_iota(jnp.int32, shape, dim)


def dot(a, b):
    return jnp.dot(a, b, preferred_element_type=f32)


def one_hot():
    k, c = iota((256, COLS), 0), iota((256, COLS), 1)
    return ((k & 127) == (c >> 6)).astype(f32).astype(bf16)


def split2(v):
    hi = v.astype(bf16)
    lo = (v - hi.astype(f32)).astype(bf16)
    return jnp.concatenate([hi, lo], axis=1)


def running_sum(rates):
    lower = (iota((TOK, TOK), 0) >= iota((TOK, TOK), 1)).astype(f32).astype(bf16)
    return dot(lower, rates)


def widen(v):
    return jnp.concatenate([v, jnp.zeros((v.shape[0], 128 - HEADS), v.dtype)], axis=1)


def state_kernel(x_ref, dt_ref, rate_ref, in_ref, *rest):
    outs, (w_ref, tot_ref, bt_ref, oh_ref) = rest[: len(PARTS)], rest[len(PARTS):]
    g = pl.program_id(0)

    @pl.when(g == 0)
    def _():
        c = running_sum(widen(rate_ref[...]))
        total = c[TOK - 1:TOK, :]
        w_ref[...] = jnp.exp(c - total) * widen(dt_ref[...]).astype(f32)
        tot_ref[...] = jnp.broadcast_to(total, (8, 128))
        bt_ref[...] = in_ref[...].astype(f32).T.astype(bf16)
        oh_ref[...] = one_hot()

    lane = iota((8, 128), 1)
    for i in range(BPS):
        b = g * BPS + i
        back = lax.rem(128 - HB * b, 128)
        w = dot(split2(pltpu.roll(w_ref[...], back, 1)), oh_ref[...])
        xs = (w * x_ref[:, i * COLS:(i + 1) * COLS].astype(f32)).astype(bf16)
        s = dot(bt_ref[...], xs).astype(bf16)
        for (j0, j1), out in zip(PARTS, outs):
            for a in range(NA):
                for j in range(j0, j1):
                    out[a, i, (j - j0) * ROWS:(j - j0 + 1) * ROWS, :] = s[
                        a * ROWS:(a + 1) * ROWS, j * 128:(j + 1) * 128]
        sums = pieces(pltpu.roll(tot_ref[...], back, 1), lane)
        for a in range(NA):
            n = (PARTS[0][1] - PARTS[0][0]) * ROWS
            outs[0][a, i, n:n + DEC, :] = sums


def pieces(total, lane):
    hi = total.astype(bf16).astype(f32)
    mid = (total - hi).astype(bf16).astype(f32)
    lo = total - hi - mid
    out = jnp.where(lane < HB, hi, 0.0)
    out = jnp.where((lane >= HB) & (lane < 2 * HB), pltpu.roll(mid, HB, 1), out)
    out = jnp.where((lane >= 2 * HB) & (lane < 3 * HB), pltpu.roll(lo, 2 * HB, 1), out)
    return out.astype(bf16)


def spread(part):
    j0, j1 = part
    k, c = iota((128, (j1 - j0) * 128), 0), iota((128, (j1 - j0) * 128), 1)
    h = (c >> 6) + 2 * j0
    return ((k == h) | (k == h + HB) | (k == h + 2 * HB)).astype(f32).astype(bf16)


def decays(ref, row, part, store):
    n = ref.shape[0]
    rows = ref[:, row:row + DEC, :].astype(f32).reshape(n * DEC, 128)
    store[...] = jnp.exp(-dot(rows.astype(bf16), spread(part)))


def two(v):
    return jnp.concatenate([v, v], axis=0)


def total_kernel(part, s_ref, first_ref, out_ref, dec_ref):
    j0, j1 = part
    nj = j1 - j0
    chunks = s_ref.shape[0]
    drow = (PARTS[0][1] - PARTS[0][0]) * ROWS
    decays(first_ref, drow, part, dec_ref)

    def step(c, total):
        at = pl.ds(pl.multiple_of(c * 8, 8), 8)
        return tuple(
            total[j] * two(dec_ref[at, j * 128:(j + 1) * 128])
            + s_ref[c, j * ROWS:(j + 1) * ROWS, :].astype(f32)
            for j in range(nj)
        )

    total = lax.fori_loop(0, chunks, step, tuple(jnp.zeros((ROWS, 128), f32) for _ in range(nj)), unroll=8)
    sums = jnp.zeros((8, 128), f32)
    for c in range(chunks):
        sums = sums + first_ref[c, drow:drow + DEC, :].astype(f32)
    lane = iota((8, 128), 1)
    whole = sums + pltpu.roll(sums, 128 - HB, 1) + pltpu.roll(sums, 128 - 2 * HB, 1)
    sums = pieces(whole, lane)
    for z in range(out_ref.shape[0]):
        for j in range(nj):
            out_ref[z, j * ROWS:(j + 1) * ROWS, :] = total[j].astype(bf16)
        out_ref[z, nj * ROWS:nj * ROWS + DEC, :] = sums


def enter_kernel(part, s_ref, first_ref, u_ref, z_ref, out_ref, dec_ref, udec_ref):
    j0, j1 = part
    nj = j1 - j0
    chunks = s_ref.shape[0]
    drow = (PARTS[0][1] - PARTS[0][0]) * ROWS
    decays(first_ref, drow, part, dec_ref)
    decays(u_ref, nj * ROWS, part, udec_ref)
    mine = z_ref[0]
    state = tuple(jnp.zeros((ROWS, 128), f32) for _ in range(nj))
    for z in range(u_ref.shape[0] - 1):
        state = tuple(
            jnp.where(
                z < mine,
                state[j] * two(udec_ref[z * 8:z * 8 + 8, j * 128:(j + 1) * 128])
                + u_ref[z, j * ROWS:(j + 1) * ROWS, :].astype(f32),
                state[j],
            )
            for j in range(nj)
        )

    def step(c, state):
        at = pl.ds(pl.multiple_of(c * 8, 8), 8)
        for j in range(nj):
            out_ref[c, j * ROWS:(j + 1) * ROWS, :] = state[j].astype(bf16)
        return tuple(
            state[j] * two(dec_ref[at, j * 128:(j + 1) * 128])
            + s_ref[c, j * ROWS:(j + 1) * ROWS, :].astype(f32)
            for j in range(nj)
        )

    lax.fori_loop(0, chunks, step, state, unroll=8)


def output_kernel(x_ref, dt_ref, rate_ref, in_ref, map_ref, gain_ref, *rest):
    hs = rest[: len(PARTS)]
    out_ref, b_ref, a_ref, e_ref, g_ref, oh_ref = rest[len(PARTS):]
    g = pl.program_id(0)

    @pl.when(g == 0)
    def _():
        c = running_sum(widen(rate_ref[...]))
        mid = c[TOK // 2 - 1:TOK // 2, :]
        b_ref[...] = jnp.exp(c - mid) * widen(dt_ref[...]).astype(f32)
        a_ref[...] = jnp.exp(mid - c)
        e_ref[...] = jnp.exp(-c)
        score = lax.dot_general(map_ref[...], in_ref[...], (((1,), (1,)), ((), ())), preferred_element_type=f32)
        g_ref[...] = jnp.where(iota((TOK, TOK), 0) >= iota((TOK, TOK), 1), score, 0.0).astype(bf16)
        oh_ref[...] = one_hot()

    for i in range(BPS):
        b = g * BPS + i
        back = lax.rem(128 - HB * b, 128)
        cols = slice(i * COLS, (i + 1) * COLS)
        x = x_ref[:, cols].astype(f32)
        oh = oh_ref[...]
        xs = (dot(split2(pltpu.roll(b_ref[...], back, 1)), oh) * x).astype(bf16)
        inner = dot(g_ref[...], xs)
        entering = jnp.concatenate(
            [
                jnp.concatenate([hs[p][a, i, (j - j0) * ROWS:(j - j0 + 1) * ROWS, :] for a in range(NA)], axis=0)
                for p, (j0, j1) in enumerate(PARTS)
                for j in range(j0, j1)
            ],
            axis=1,
        )
        carried = dot(map_ref[...], entering)
        gain = dot(split2(pltpu.roll(gain_ref[...], back, 1)), oh)[0:1, :]
        result = gain * x
        result = result + dot(split2(pltpu.roll(a_ref[...], back, 1)), oh) * inner
        result = result + dot(split2(pltpu.roll(e_ref[...], back, 1)), oh) * carried
        out_ref[:, cols] = result.astype(bf16)


def whole(shape):
    return pl.BlockSpec(shape, lambda *g: (0,) * len(shape))


def params():
    return pltpu.CompilerParams(vmem_limit_bytes=48 * 1024 * 1024)


def local(x, dt, rate, in_map, out_map, gain):
    nz, nw, ny = lax.axis_size("z"), lax.axis_size("w"), lax.axis_size("y")
    chunks = nw * ny
    rows = [(j1 - j0) * ROWS for j0, j1 in PARTS]
    srows = [r + (DEC if p == 0 else 0) for p, r in enumerate(rows)]
    xspec = pl.BlockSpec((TOK, BPS * COLS), lambda g: (0, g))
    small = [whole((TOK, HEADS)), whole((TOK, HEADS)), whole((TOK, STATE))]

    def pieces_spec(r):
        return pl.BlockSpec((NA, BPS, r, 128), lambda g: (0, g, 0, 0))

    sent = pl.pallas_call(
        state_kernel,
        grid=(STEPS,),
        in_specs=[xspec] + small,
        out_specs=[pieces_spec(r) for r in srows],
        out_shape=[jax.ShapeDtypeStruct((NA, NB, r, 128), bf16) for r in srows],
        scratch_shapes=[
            pltpu.VMEM((TOK, 128), f32),
            pltpu.VMEM((8, 128), f32),
            pltpu.VMEM((STATE, TOK), bf16),
            pltpu.VMEM((256, COLS), bf16),
        ],
        compiler_params=params(),
        name="chunk_states",
    )(x, dt, rate, in_map)
    got = [
        lax.all_to_all(s.reshape(chunks, r, 128), ("w", "y"), 0, 0, tiled=True) for s, r in zip(sent, srows)
    ]
    mine = lax.axis_index("z").astype(jnp.int32).reshape(1)
    back = []
    for part, s, r in zip(PARTS, got, rows):
        cols = (part[1] - part[0]) * 128
        totals = pl.pallas_call(
            functools.partial(total_kernel, part),
            out_shape=jax.ShapeDtypeStruct((nz, r + DEC, 128), bf16),
            scratch_shapes=[pltpu.VMEM((chunks * 8, cols), f32)],
            compiler_params=params(),
            name="block_total",
        )(s, got[0])
        totals = lax.all_to_all(totals, "z", 0, 0, tiled=True)
        entering = pl.pallas_call(
            functools.partial(enter_kernel, part),
            in_specs=[pl.BlockSpec(memory_space=pltpu.VMEM)] * 3 + [pl.BlockSpec(memory_space=pltpu.SMEM)],
            out_shape=jax.ShapeDtypeStruct((chunks, r, 128), bf16),
            scratch_shapes=[pltpu.VMEM((chunks * 8, cols), f32), pltpu.VMEM((nz * 8, cols), f32)],
            compiler_params=params(),
            name="entering_states",
        )(s, got[0], totals, mine)
        back.append(lax.all_to_all(entering, ("w", "y"), 0, 0, tiled=True).reshape(NA, NB, r, 128))
    gains = jnp.broadcast_to(jnp.pad(gain, (0, 128 - HEADS))[None, :], (8, 128))
    return pl.pallas_call(
        output_kernel,
        grid=(STEPS,),
        in_specs=[xspec] + small + [whole((TOK, STATE)), whole((8, 128))] + [pieces_spec(r) for r in rows],
        out_specs=xspec,
        out_shape=jax.ShapeDtypeStruct(x.shape, bf16),
        scratch_shapes=[pltpu.VMEM((TOK, 128), f32)] * 3
        + [pltpu.VMEM((TOK, TOK), bf16), pltpu.VMEM((256, COLS), bf16)],
        compiler_params=params(),
        name="outputs",
    )(x, dt, rate, in_map, out_map, gains, *back)


def solution(mesh):
    ny = mesh.shape["head"]
    nw = 64 // ny
    axes = ("z", "w", "y")
    cut = Mesh(mesh.devices.reshape(-1, nw, ny), axes)
    split = P(axes, None)
    return jax.shard_map(
        local,
        mesh=cut,
        in_specs=(split, split, split, split, split, P()),
        out_specs=split,
        check_vma=False,
    )
```

time: 490 us -> 125 us (0.26)
  blocking collectives: 247 us -> 48.1 us
  local copies, waits for them, and re-layouts: 92.1 us -> 4.82 us
  other arithmetic: 76 us -> 0 us
  waiting for transfers between devices: 10 us -> 42.6 us
  matrix products: 28.6 us -> 0 us
  between operations: 14.4 us -> 0.08 us
  Pallas kernels: 0 us -> 10.8 us
    unnamed x1 -> x0, blocking collectives: 144 us -> none
    select_n x63 -> x0, other arithmetic: 68.2 us -> none  [lap(): jnp.where(position < mine, new, old)]
    dynamic_update_slice x8 -> x0, local copies, waits for them, and re-layouts: 63 us -> none  [local(): lax.scan(advance, (start_state, start_offset), pieces)]
    all_gather x2 -> x0, blocking collectives: 62.7 us -> none  [the longest x1 43.4 us: local(): lax.all_gather(output_map, 'head', axis=0, tiled=True)]
    all_to_all x3 -> x2, waiting for transfers between devices: 9.97 us -> 42.6 us  [the longest x1 33.6 us: local(): lax.all_to_all(entering, ('w', 'y'), 0, 0, tiled=True)]
    dot_general x17 -> x0, matrix products: 28.6 us -> none  [the longest x4 12.4 us: ssd_block(): jnp.einsum('tsh,shp->thp', weights * intersections[:, :, None], scaled, p...]
    pallas_call x0 -> x4, Pallas kernels: none -> 10.8 us  [the longest x1 5.48 us: local(): pl.pallas_call(output_kernel, grid=(STEPS,), in_specs=[xspec] + small + [...]
    dynamic_slice x17 -> x0, local copies, waits for them, and re-layouts: 10.5 us -> none  [the longest x16 9.83 us: local(): lax.scan(advance, (start_state, start_offset), pieces)]
  transfers between devices with their start and end apart: 4 -> 2, of which waited for: 2 -> 2; matrix products, arithmetic and copies ran while one was open for 2% -> 0% of each run, Pallas kernels for 0% -> 0%
where the time goes in v1:
time: 125 us
  blocking collectives  48.1 us (38%)
  waiting for transfers between devices  42.6 us (34%)
  starting transfers between devices  18.3 us (15%)
  Pallas kernels  10.8 us (9%)
  local copies, waits for them, and re-layouts  4.82 us (4%)
    all_to_all x1, blocking collectives, local(): lax.all_to_all(s.reshape(chunks, r, 128), ('w', 'y'), 0, 0, tiled=True)  48.1 us
    all_to_all x1, waiting for transfers between devices, local(): lax.all_to_all(entering, ('w', 'y'), 0, 0, tiled=True)  33.6 us
    all_to_all x1, starting transfers between devices, local(): totals = lax.all_to_all(totals, 'z', 0, 0, tiled=True)  10 us
    all_to_all x1, waiting for transfers between devices, local(): totals = lax.all_to_all(totals, 'z', 0, 0, tiled=True)  9.01 us
    all_to_all x1, starting transfers between devices, local(): lax.all_to_all(entering, ('w', 'y'), 0, 0, tiled=True)  8.23 us
    pallas_call x1, Pallas kernels, local(): pl.pallas_call(output_kernel, grid=(STEPS,), in_specs=[xspec] + small + [...  5.48 us
    unnamed x16, local copies, waits for them, and re-layouts  4.81 us
    pallas_call x1, Pallas kernels, local(): pl.pallas_call(state_kernel, grid=(STEPS,), in_specs=[xspec] + small, out...  2.96 us
  transfers between devices with their start and end apart: 2, of which 2 were waited for; matrix products, arithmetic and copies ran while one was open for 0% of the time, Pallas kernels for 0%

profile of v1, /device:TPU:1, one launch (start us, length us, event | category | flops | bytes accessed | tf_op | source)
XLA Modules:
  0.0 124.7 jit_solution(5280559185996657006)
XLA Ops:
  0.0 0.8 copy.10.rate_ref
  0.8 0.8 copy.9.dt_ref
  1.7 0.0 copy-start
  1.7 1.3 %copy-done = bf16[128,5120]{1,0:T(8,128)(2,1)S(1)} copy-done((bf16[128,5120]{1,0:T(8,128)(2,1)S(1)}, bf16[128,5120]{1,0:T(8,128)(2,1)}, u32[]{:S(2)}) %copy-start) | copy-done | bytes 1310744
  3.0 0.0 copy-start.3
  3.0 0.8 copy-done.3
  3.8 3.0 %chunk_states.1 = bf16[8,8,88,128]{3,2,1,0:T(8,128)(2,1)S(1)} custom-call(bf16[128,5120]{1,0:T(8,128)(2,1)S(1)} %copy-done, bf16[128,80]{1,0:T(8,128)(2,1)S(1)} %copy.9.dt_ref, bf16[128,80]{1,0:T(8,128)(2,1)S(1)} %copy.10.rate_ref, bf16[128,128]{1,0:T(8,128)(2,1)S(1)} %copy-done.3), custom_call_target="tpu_custom_call" | custom-call | tf_op jit(solution)/shard_map/chunk_states/pallas_call | solution.py:235
  6.7 48.1 %all_to_all.15.s_ref.first_ref = bf16[64,88,128]{2,1,0:T(8,128)(2,1)S(1)} all-to-all(bf16[64,88,128]{2,1,0:T(8,128)(2,1)S(1)} %bitcast.3), channel_id=1, replica_groups=mesh['z'=8,'w'=8,'y'=8] {'w','y'}, dimensions={0} | all-to-all | bytes 2883584 | tf_op jit(solution)/shard_map/all_to_all | solution.py:251
  54.8 1.6 %block_total.1 = bf16[8,88,128]{2,1,0:T(8,128)(2,1)} custom-call(bf16[64,88,128]{2,1,0:T(8,128)(2,1)S(1)} %all_to_all.15.s_ref.first_ref, bf16[64,88,128]{2,1,0:T(8,128)(2,1)S(1)} %all_to_all.15.s_ref.first_ref), custom_call_target="tpu_custom_call" | custom-call | tf_op jit(solution)/shard_map/block_total/pallas_call | solution.py:257
  56.4 10.0 %all-to-all-start.1 = ((bf16[8,88,128]{2,1,0:T(8,128)(2,1)}), bf16[8,88,128]{2,1,0:T(8,128)(2,1)S(1)}, u32[]{:S(2)}, u32[]{:S(2)}) async-start(bf16[8,88,128]{2,1,0:T(8,128)(2,1)} %block_total.1), calls=%async_computation.1 | async-start | bytes 360448 | tf_op jit(solution)/shard_map/all_to_all | solution.py:264
  66.4 9.0 %all-to-all-done.1.u_ref = bf16[8,88,128]{2,1,0:T(8,128)(2,1)S(1)} async-done(((bf16[8,88,128]{2,1,0:T(8,128)(2,1)}), bf16[8,88,128]{2,1,0:T(8,128)(2,1)S(1)}, u32[]{:S(2)}, u32[]{:S(2)}) %all-to-all-start.1) | async-done | bytes 180256 | tf_op jit(solution)/shard_map/all_to_all | solution.py:264
  75.4 0.8 entering_states.1
  76.2 0.0 copy-start.2
  76.2 1.0 copy-done.2
  77.3 0.0 copy-start.6
  77.3 0.0 copy-start.1
  77.3 0.0 copy-start.4
  77.3 0.0 copy-start.5
  77.3 8.2 %all-to-all-start.2 = ((bf16[64,80,128]{2,1,0:T(8,128)(2,1)}), bf16[64,80,128]{2,1,0:T(8,128)(2,1)S(1)}, u32[]{:S(2)}, u32[]{:S(2)}) async-start(bf16[64,80,128]{2,1,0:T(8,128)(2,1)} %copy-done.2), calls=%async_computation.2 | async-start | bytes 2621440 | tf_op jit(solution)/shard_map/all_to_all | solution.py:273
  85.5 0.0 copy-done.6
  85.6 33.6 %all-to-all-done.2 = bf16[64,80,128]{2,1,0:T(8,128)(2,1)S(1)} async-done(((bf16[64,80,128]{2,1,0:T(8,128)(2,1)}), bf16[64,80,128]{2,1,0:T(8,128)(2,1)S(1)}, u32[]{:S(2)}, u32[]{:S(2)}) %all-to-all-start.2) | async-done | bytes 1310752 | tf_op jit(solution)/shard_map/all_to_all | solution.py:273
  119.2 0.0 copy-done.1
  119.2 0.0 copy-done.4
  119.2 0.0 copy-done.5
  119.2 5.5 %outputs.1 = bf16[128,5120]{1,0:T(8,128)(2,1)} custom-call(bf16[128,5120]{1,0:T(8,128)(2,1)S(1)} %copy-done.1, bf16[128,80]{1,0:T(8,128)(2,1)S(1)} %copy.9.dt_ref, bf16[128,80]{1,0:T(8,128)(2,1)S(1)} %copy.10.rate_ref, bf16[128,128]{1,0:T(8,128)(2,1)S(1)} %copy-done.4, bf16[128,128]{1,0:T(8,128)(2,1)S(1)} %copy-done.5, ...), custom_call_target="tpu_custom_call" | custom-call | tf_op jit(solution)/shard_map/outputs/pallas_call | solution.py:275
  (2 shorter events, 0.0 us)
Async XLA Ops:
  1.7 1.3 %copy-start = (bf16[128,5120]{1,0:T(8,128)(2,1)S(1)}, bf16[128,5120]{1,0:T(8,128)(2,1)}, u32[]{:S(2)}) copy-start(bf16[128,5120]{1,0:T(8,128)(2,1)} %x_ref.3) | copy-start | bytes 3932164
  3.0 0.8 copy-start.3
  56.4 19.0 %all-to-all-start.1 = ((bf16[8,88,128]{2,1,0:T(8,128)(2,1)}), bf16[8,88,128]{2,1,0:T(8,128)(2,1)S(1)}, u32[]{:S(2)}, u32[]{:S(2)}) async-start(bf16[8,88,128]{2,1,0:T(8,128)(2,1)} %block_total.1), calls=%async_computation.1 | async-start | bytes 360448 | tf_op jit(solution)/shard_map/all_to_all | solution.py:264
  76.2 1.1 copy-start.2
  77.3 8.3 %copy-start.6 = (f32[80]{0:T(128)S(1)}, f32[80]{0:T(128)}, u32[]{:S(2)}) copy-start(f32[80]{0:T(128)} %param.11) | copy-start | bytes 964
  77.3 41.9 %copy-start.1 = (bf16[128,5120]{1,0:T(8,128)(2,1)S(1)}, bf16[128,5120]{1,0:T(8,128)(2,1)}, u32[]{:S(2)}) copy-start(bf16[128,5120]{1,0:T(8,128)(2,1)} %x_ref.3) | copy-start | bytes 3932164
  77.3 41.9 %copy-start.4 = (bf16[128,128]{1,0:T(8,128)(2,1)S(1)}, bf16[128,128]{1,0:T(8,128)(2,1)}, u32[]{:S(2)}) copy-start(bf16[128,128]{1,0:T(8,128)(2,1)} %in_ref.3) | copy-start | bytes 98308
  77.3 41.9 %copy-start.5 = (bf16[128,128]{1,0:T(8,128)(2,1)S(1)}, bf16[128,128]{1,0:T(8,128)(2,1)}, u32[]{:S(2)}) copy-start(bf16[128,128]{1,0:T(8,128)(2,1)} %map_ref.1) | copy-start | bytes 98308
  77.3 41.9 %all-to-all-start.2 = ((bf16[64,80,128]{2,1,0:T(8,128)(2,1)}), bf16[64,80,128]{2,1,0:T(8,128)(2,1)S(1)}, u32[]{:S(2)}, u32[]{:S(2)}) async-start(bf16[64,80,128]{2,1,0:T(8,128)(2,1)} %copy-done.2), calls=%async_computation.2 | async-start | bytes 2621440 | tf_op jit(solution)/shard_map/all_to_all | solution.py:273

commit v2 on v1

v2 whole, which is shorter than its diff:
```python
import functools

import jax
import jax.numpy as jnp
from jax import lax
from jax.experimental import pallas as pl
from jax.experimental.pallas import tpu as pltpu
from jax.sharding import Mesh
from jax.sharding import PartitionSpec as P

HEADS = 80
HEAD_DIM = 64
STATE = 128
TOK = 128
HB = 10
COLS = HB * HEAD_DIM
NB = HEADS // HB
NA = 8
ROWS = STATE // NA
TILES = COLS // 128
DEC = 8
STEPS = 4
BPS = NB // STEPS
GROUP = NA * NB
ROWS_H = TILES * ROWS
ROWS_S = ROWS_H + DEC

f32, bf16 = jnp.float32, jnp.bfloat16


def iota(shape, dim):
    return lax.broadcasted_iota(jnp.int32, shape, dim)


def dot(a, b):
    return jnp.dot(a, b, preferred_element_type=f32)


def one_hot():
    k, c = iota((256, COLS), 0), iota((256, COLS), 1)
    return ((k & 127) == (c >> 6)).astype(f32).astype(bf16)


def split2(v):
    hi = v.astype(bf16)
    lo = (v - hi.astype(f32)).astype(bf16)
    return jnp.concatenate([hi, lo], axis=1)


def across(matrix, heads_first):
    v = lax.dot_general(matrix, heads_first, (((1,), (1,)), ((), ())), preferred_element_type=f32)
    return jnp.concatenate([v, jnp.zeros((TOK, 128 - HEADS), f32)], axis=1)


def sums_and_steps(rate_ref, dt_ref):
    same = (iota((TOK, TOK), 0) == iota((TOK, TOK), 1)).astype(f32).astype(bf16)
    return across(triangle(), rate_ref[...]), across(same, dt_ref[...])


def triangle(upper=False):
    row, column = iota((TOK, TOK), 0), iota((TOK, TOK), 1)
    keep = row <= column if upper else row >= column
    return keep.astype(f32).astype(bf16)


def columns(b):
    return slice(b * COLS, (b + 1) * COLS)


def state_kernel(x_ref, dt_ref, rate_ref, in_ref, out_ref, x_buf, x_sems, w_ref, bt_ref):
    def load(b):
        return pltpu.make_async_copy(x_ref.at[:, columns(b)], x_buf.at[b], x_sems.at[b])

    for b in range(NB):
        load(b).start()
    rate = rate_ref[...]
    c = dot(rate, triangle(upper=True))
    w_ref[...] = jnp.exp(c - c[:, TOK - 1:TOK]) * dt_ref[...].astype(f32)
    bt_ref[...] = in_ref[...].astype(f32).T
    total = lax.dot_general(
        jnp.ones((8, TOK), bf16), rate, (((1,), (1,)), ((), ())), preferred_element_type=f32)
    total = jnp.concatenate([total, jnp.zeros((8, 128 - HEADS), f32)], axis=1)
    left = iota((STATE, 128), 1) < HEAD_DIM
    lane = iota((8, 128), 1)
    for b in range(NB):
        sums = pieces(pltpu.roll(total, (128 - HB * b) % 128, 1), lane)
        load(b).wait()
        for j in range(TILES):
            h = b * HB + 2 * j
            rows = jnp.concatenate([bt_ref[...] * w_ref[h:h + 1, :], bt_ref[...] * w_ref[h + 1:h + 2, :]], axis=0)
            s = dot(rows.astype(bf16), x_buf[b, :, j * 128:(j + 1) * 128])
            s = jnp.where(left, s[:STATE], s[STATE:]).astype(bf16)
            for a in range(NA):
                out_ref[a, b, j * ROWS:(j + 1) * ROWS, :] = s[a * ROWS:(a + 1) * ROWS, :]
        for a in range(NA):
            out_ref[a, b, ROWS_H:ROWS_S, :] = sums


def pieces(total, lane):
    hi = total.astype(bf16).astype(f32)
    mid = (total - hi).astype(bf16).astype(f32)
    lo = total - hi - mid
    out = jnp.where(lane < HB, hi, 0.0)
    out = jnp.where((lane >= HB) & (lane < 2 * HB), pltpu.roll(mid, HB, 1), out)
    out = jnp.where((lane >= 2 * HB) & (lane < 3 * HB), pltpu.roll(lo, 2 * HB, 1), out)
    return out.astype(bf16)


def decays(ref, store):
    k, c = iota((128, COLS), 0), iota((128, COLS), 1)
    h = c >> 6
    spread = ((k == h) | (k == h + HB) | (k == h + 2 * HB)).astype(f32).astype(bf16)
    rows = ref[:, ROWS_H:ROWS_S, :].astype(f32).reshape(ref.shape[0] * DEC, 128).astype(bf16)
    store[...] = jnp.exp(-dot(rows, spread))
    return rows


def two(v):
    return jnp.concatenate([v, v], axis=0)


def zeros():
    return tuple(jnp.zeros((ROWS, 128), f32) for _ in range(TILES))


def follow(state, ref, at, dec_ref, row):
    rows = slice(row * 8, row * 8 + 8) if isinstance(row, int) else pl.ds(pl.multiple_of(row * 8, 8), 8)
    return tuple(
        state[j] * two(dec_ref[rows, j * 128:(j + 1) * 128]) + ref[at, j * ROWS:(j + 1) * ROWS, :].astype(f32)
        for j in range(TILES)
    )


def total_kernel(s_ref, out_ref, dec_ref):
    rows = decays(s_ref, dec_ref)
    sums = dot(jnp.full((8, GROUP * DEC), 1 / DEC, bf16), rows)
    sums = sums + pltpu.roll(sums, 128 - HB, 1) + pltpu.roll(sums, 128 - 2 * HB, 1)
    sums = pieces(sums, iota((8, 128), 1))
    total = lax.fori_loop(0, GROUP, lambda c, t: follow(t, s_ref, c, dec_ref, c), zeros(), unroll=8)
    for z in range(out_ref.shape[0]):
        for j in range(TILES):
            out_ref[z, j * ROWS:(j + 1) * ROWS, :] = total[j].astype(bf16)
        out_ref[z, ROWS_H:ROWS_S, :] = sums


def enter_kernel(s_ref, u_ref, z_ref, out_ref, dec_ref, udec_ref, out_buf, sems):
    decays(s_ref, dec_ref)
    decays(u_ref, udec_ref)
    mine = z_ref[0]
    state = zeros()
    for z in range(u_ref.shape[0] - 1):
        later = follow(state, u_ref, z, udec_ref, z)
        state = tuple(jnp.where(z < mine, new, old) for new, old in zip(later, state))

    def store(g):
        return pltpu.make_async_copy(out_buf.at[pl.ds(g * NB, NB)], out_ref.at[pl.ds(g * NB, NB)], sems.at[g])

    def group(g, state):
        for i in range(NB):
            c = g * NB + i
            for j in range(TILES):
                out_buf[c, j * ROWS:(j + 1) * ROWS, :] = state[j].astype(bf16)
            state = follow(state, s_ref, c, dec_ref, c)
        store(g).start()
        return state

    lax.fori_loop(0, GROUP // NB, group, state)
    for g in range(GROUP // NB):
        store(g).wait()


def inner_kernel(x_ref, dt_ref, rate_ref, in_ref, map_ref, gain_ref, out_ref, b_ref, a_ref, g_ref, oh_ref):
    g = pl.program_id(0)

    @pl.when(g == 0)
    def _():
        c, dt = sums_and_steps(rate_ref, dt_ref)
        mid = c[TOK // 2 - 1:TOK // 2, :]
        b_ref[...] = jnp.exp(c - mid) * dt
        a_ref[...] = jnp.exp(mid - c)
        score = lax.dot_general(map_ref[...], in_ref[...], (((1,), (1,)), ((), ())), preferred_element_type=f32)
        g_ref[...] = jnp.where(iota((TOK, TOK), 0) >= iota((TOK, TOK), 1), score, 0.0).astype(bf16)
        oh_ref[...] = one_hot()

    for i in range(BPS):
        back = lax.rem(128 - HB * (g * BPS + i), 128)
        cols = slice(i * COLS, (i + 1) * COLS)
        x = x_ref[:, cols].astype(f32)
        oh = oh_ref[...]
        xs = (dot(split2(pltpu.roll(b_ref[...], back, 1)), oh) * x).astype(bf16)
        gain = dot(split2(pltpu.roll(gain_ref[...], back, 1)), oh)[0:1, :]
        weight = dot(split2(pltpu.roll(a_ref[...], back, 1)), oh)
        out_ref[:, cols] = gain * x + weight * dot(g_ref[...], xs)


def output_kernel(part_ref, rate_ref, map_ref, h_ref, out_ref, h_buf, out_buf, h_sems, out_sems, weight_buf):
    def load(b):
        return pltpu.make_async_copy(h_ref.at[:, b], h_buf.at[b], h_sems.at[b])

    def store(b):
        return pltpu.make_async_copy(out_buf.at[b], out_ref.at[:, columns(b)], out_sems.at[b])

    for b in range(NB):
        load(b).start()
    decay = jnp.exp(-across(triangle(), rate_ref[...]))
    oh = one_hot()
    for b in range(NB):
        weight_buf[b] = dot(split2(pltpu.roll(decay, (128 - HB * b) % 128, 1)), oh)
    for b in range(NB):
        load(b).wait()
        entering = jnp.concatenate(
            [
                jnp.concatenate([h_buf[b, a, j * ROWS:(j + 1) * ROWS, :] for a in range(NA)], axis=0)
                for j in range(TILES)
            ],
            axis=1,
        )
        carried = weight_buf[b] * dot(map_ref[...], entering)
        out_buf[b] = (part_ref[:, columns(b)] + carried).astype(bf16)
        store(b).start()
    for b in range(NB):
        store(b).wait()


def whole(shape):
    return pl.BlockSpec(shape, lambda *g: (0,) * len(shape))


def params():
    return pltpu.CompilerParams(vmem_limit_bytes=16 << 20)


def cost(us):
    return pl.CostEstimate(flops=0, bytes_accessed=us * 3000000, transcendentals=0)


def local(x, dt, rate, in_map, out_map, gain):
    nz = lax.axis_size("d") // GROUP
    near = [[z * GROUP + p for p in range(GROUP)] for z in range(nz)]
    far = [[z * GROUP + p for z in range(nz)] for p in range(GROUP)]
    exchange = functools.partial(lax.all_to_all, axis_name="d", split_axis=0, concat_axis=0, tiled=True)
    dt, rate = dt.T, rate.T
    xspec = pl.BlockSpec((TOK, BPS * COLS), lambda g: (0, g))
    small = [whole((HEADS, TOK)), whole((HEADS, TOK)), whole((TOK, STATE))]
    matrix = pltpu.VMEM((TOK, 128), f32)
    hot = pltpu.VMEM((256, COLS), bf16)

    vmem, hbm = pl.BlockSpec(memory_space=pltpu.VMEM), pl.BlockSpec(memory_space=pl.ANY)
    sems = pltpu.SemaphoreType.DMA((NB,))
    sent = pl.pallas_call(
        state_kernel,
        in_specs=[pl.BlockSpec(memory_space=pltpu.HBM), vmem, vmem, vmem],
        out_specs=vmem,
        out_shape=pltpu.VMEM((NA, NB, ROWS_S, 128), bf16),
        scratch_shapes=[
            pltpu.VMEM((NB, TOK, COLS), bf16),
            sems,
            pltpu.VMEM((HEADS, TOK), f32),
            pltpu.VMEM((STATE, TOK), f32),
        ],
        compiler_params=pltpu.CompilerParams(vmem_limit_bytes=56 << 20),
        name="chunk_states",
    )(x, dt, rate, in_map)
    states = exchange(sent.reshape(GROUP, ROWS_S, 128), axis_index_groups=near)
    totals = pl.pallas_call(
        total_kernel,
        out_shape=jax.ShapeDtypeStruct((nz, ROWS_S, 128), bf16),
        scratch_shapes=[pltpu.VMEM((GROUP * DEC, COLS), f32)],
        compiler_params=params(),
        name="block_total",
    )(states)
    totals = exchange(totals, axis_index_groups=far)
    entering = pl.pallas_call(
        enter_kernel,
        in_specs=[vmem, vmem, pl.BlockSpec(memory_space=pltpu.SMEM)],
        out_specs=hbm,
        out_shape=jax.ShapeDtypeStruct((GROUP, ROWS_H, 128), bf16),
        scratch_shapes=[
            pltpu.VMEM((GROUP * DEC, COLS), f32),
            pltpu.VMEM((nz * DEC, COLS), f32),
            pltpu.VMEM((GROUP, ROWS_H, 128), bf16),
            pltpu.SemaphoreType.DMA((GROUP // NB,)),
        ],
        compiler_params=params(),
        name="entering_states",
    )(states, totals, (lax.axis_index("d") // GROUP).astype(jnp.int32).reshape(1))
    entering = exchange(entering, axis_index_groups=near).reshape(NA, NB, ROWS_H, 128)
    gains = jnp.broadcast_to(jnp.pad(gain, (0, 128 - HEADS))[None, :], (8, 128))
    part = pl.pallas_call(
        inner_kernel,
        grid=(STEPS,),
        in_specs=[xspec] + small + [whole((TOK, STATE)), whole((8, 128))],
        out_specs=xspec,
        out_shape=jax.ShapeDtypeStruct(x.shape, f32),
        scratch_shapes=[matrix, matrix, pltpu.VMEM((TOK, TOK), bf16), hot],
        compiler_params=params(),
        cost_estimate=cost(4),
        name="inner_outputs",
    )(x, dt, rate, in_map, out_map, gains)
    return pl.pallas_call(
        output_kernel,
        in_specs=[vmem, vmem, vmem, hbm],
        out_specs=hbm,
        out_shape=jax.ShapeDtypeStruct(x.shape, bf16),
        scratch_shapes=[
            pltpu.VMEM((NB, NA, ROWS_H, 128), bf16),
            pltpu.VMEM((NB, TOK, COLS), bf16),
            sems,
            sems,
            pltpu.VMEM((NB, TOK, COLS), f32),
        ],
        compiler_params=params(),
        name="outputs",
    )(part, rate, out_map, entering)


def solution(mesh):
    line = Mesh(mesh.devices.reshape(-1), ("d",))
    split = P("d", None)
    return jax.shard_map(
        local,
        mesh=line,
        in_specs=(split, split, split, split, split, P()),
        out_specs=split,
        check_vma=False,
    )
```

time: 125 us -> 120 us (0.960)
  waiting for transfers between devices: 42.6 us -> 38.1 us
  local copies, waits for them, and re-layouts: 4.82 us -> 1.35 us
  Pallas kernels: 10.8 us -> 13.4 us
    all_to_all x2, waiting for transfers between devices: 42.6 us -> 38.1 us  [the longest x1 29.1 us: local(): exchange(entering, axis_index_groups=near).reshape(NA, NB, ROWS_H, 128)]
    unnamed x16 -> x12, local copies, waits for them, and re-layouts: 4.81 us -> 1.34 us
    pallas_call x4 -> x5, Pallas kernels: 10.8 us -> 13.4 us  [the longest x1 3.85 us: local(): pl.pallas_call(state_kernel, in_specs=[pl.BlockSpec(memory_space=pltpu.HB...]
  transfers between devices with their start and end apart: 2 -> 2, of which waited for: 2 -> 2; matrix products, arithmetic and copies ran while one was open for 0% -> 0% of each run, Pallas kernels for 0% -> 3%
where the time goes in v2:
time: 120 us; the launch traced here: 119 us
  blocking collectives  48.1 us (40%)
  waiting for transfers between devices  38.1 us (32%)
  starting transfers between devices  18.4 us (15%)
  Pallas kernels  13.4 us (11%)
  local copies, waits for them, and re-layouts  1.35 us (1%)
    all_to_all x1, blocking collectives, local(): states = exchange(sent.reshape(GROUP, ROWS_S, 128), axis_index_groups=near)  48.1 us
    all_to_all x1, waiting for transfers between devices, local(): exchange(entering, axis_index_groups=near).reshape(NA, NB, ROWS_H, 128)  29.1 us
    all_to_all x1, starting transfers between devices, local(): totals = exchange(totals, axis_index_groups=far)  10 us
    all_to_all x1, waiting for transfers between devices, local(): totals = exchange(totals, axis_index_groups=far)  9.01 us
    all_to_all x1, starting transfers between devices, local(): exchange(entering, axis_index_groups=near).reshape(NA, NB, ROWS_H, 128)  8.4 us
    pallas_call x1, Pallas kernels, local(): pl.pallas_call(state_kernel, in_specs=[pl.BlockSpec(memory_space=pltpu.HB...  3.85 us
    pallas_call x1, Pallas kernels, local(): pl.pallas_call(output_kernel, in_specs=[vmem, vmem, vmem, hbm], out_specs...  3.34 us
    pallas_call x1, Pallas kernels, local(): pl.pallas_call(inner_kernel, grid=(STEPS,), in_specs=[xspec] + small + [w...  3.1 us
  transfers between devices with their start and end apart: 2, of which 2 were waited for; matrix products, arithmetic and copies ran while one was open for 0% of the time, Pallas kernels for 3%

profile of v2, /device:TPU:1, one launch (start us, length us, event | category | flops | bytes accessed | tf_op | source)
XLA Modules:
  0.0 119.5 jit_solution(8456837221062255558)
XLA Ops:
  0.0 3.8 %chunk_states.1 = bf16[8,8,88,128]{3,2,1,0:T(8,128)(2,1)S(1)} custom-call(bf16[128,5120]{1,0:T(8,128)(2,1)} %x_ref.3, bf16[80,128]{1,0:T(8,128)(2,1)} %bitcast.9, bf16[80,128]{1,0:T(8,128)(2,1)} %bitcast.6, bf16[128,128]{1,0:T(8,128)(2,1)} %in_ref.3), custom_call_target="tpu_custom_call" | custom-call | tf_op jit(solution)/shard_map/chunk_states/pallas_call | solution.py:250
  3.9 48.1 %all_to_all.15.s_ref = bf16[64,88,128]{2,1,0:T(8,128)(2,1)S(1)} all-to-all(bf16[64,88,128]{2,1,0:T(8,128)(2,1)S(1)} %bitcast.5), channel_id=1, replica_groups={{0,1,2,3,4,5,6,7,8,9,10,11,12,13,14,15,16,17,18,19,20,21,22,23,24,25,26..., dimensions={0} | all-to-all | bytes 2883584 | tf_op jit(solution)/shard_map/all_to_all | solution.py:264
  51.9 1.5 %block_total.1 = bf16[8,88,128]{2,1,0:T(8,128)(2,1)} custom-call(bf16[64,88,128]{2,1,0:T(8,128)(2,1)S(1)} %all_to_all.15.s_ref), custom_call_target="tpu_custom_call" | custom-call | tf_op jit(solution)/shard_map/block_total/pallas_call | solution.py:265
  53.5 10.0 %all-to-all-start.1 = ((bf16[8,88,128]{2,1,0:T(8,128)(2,1)}), bf16[8,88,128]{2,1,0:T(8,128)(2,1)S(1)}, u32[]{:S(2)}, u32[]{:S(2)}) async-start(bf16[8,88,128]{2,1,0:T(8,128)(2,1)} %block_total.1), calls=%async_computation.1 | async-start | bytes 360448 | tf_op jit(solution)/shard_map/all_to_all | solution.py:272
  63.5 9.0 %all-to-all-done.1.u_ref = bf16[8,88,128]{2,1,0:T(8,128)(2,1)S(1)} async-done(((bf16[8,88,128]{2,1,0:T(8,128)(2,1)}), bf16[8,88,128]{2,1,0:T(8,128)(2,1)S(1)}, u32[]{:S(2)}, u32[]{:S(2)}) %all-to-all-start.1) | async-done | bytes 180256 | tf_op jit(solution)/shard_map/all_to_all | solution.py:272
  72.5 1.6 %entering_states.1 = bf16[64,80,128]{2,1,0:T(8,128)(2,1)} custom-call(bf16[64,88,128]{2,1,0:T(8,128)(2,1)S(1)} %all_to_all.15.s_ref, bf16[8,88,128]{2,1,0:T(8,128)(2,1)S(1)} %all-to-all-done.1.u_ref, s32[1]{0:T(128)} %bitcast.3.z_ref), custom_call_target="tpu_custom_call" | custom-call | tf_op jit(solution)/shard_map/entering_states/pallas_call | solution.py:273
  74.1 0.0 copy-start.5
  74.1 0.0 copy-start.1
  74.1 0.0 copy-start.2
  74.1 0.0 copy-start.3
  74.1 0.0 copy-start.4
  74.2 8.4 %all-to-all-start.2 = ((bf16[64,80,128]{2,1,0:T(8,128)(2,1)}), bf16[64,80,128]{2,1,0:T(8,128)(2,1)}, u32[]{:S(2)}, u32[]{:S(2)}) async-start(bf16[64,80,128]{2,1,0:T(8,128)(2,1)} %entering_states.1), calls=%async_computation.2 | async-start | bytes 2621440 | tf_op jit(solution)/shard_map/all_to_all | solution.py:287
  82.6 0.0 copy-done.5
  82.6 0.0 copy-done.1
  82.6 0.0 copy-done.2
  82.6 0.0 copy-done.3
  82.6 0.0 copy-done.4
  82.6 0.0 copy-start
  82.7 1.3 %copy-done = bf16[128,5120]{1,0:T(8,128)(2,1)S(1)} copy-done((bf16[128,5120]{1,0:T(8,128)(2,1)S(1)}, bf16[128,5120]{1,0:T(8,128)(2,1)}, u32[]{:S(2)}) %copy-start) | copy-done | bytes 1310744
  84.0 3.1 %inner_outputs.1.part_ref = f32[128,5120]{1,0:T(8,128)S(1)} custom-call(bf16[128,5120]{1,0:T(8,128)(2,1)S(1)} %copy-done, bf16[80,128]{1,0:T(8,128)(2,1)S(1)} %bitcast.10, bf16[80,128]{1,0:T(8,128)(2,1)S(1)} %bitcast.7, bf16[128,128]{1,0:T(8,128)(2,1)S(1)} %copy-done.2, bf16[128,128]{1,0:T(8,128)(2,1)S(1)} %copy-done.3, f32[8,128]{1,0:T(8,128)S(1)} %broadcast_in_dim.2.gain_ref), custom_call_target="tpu_custom_call" | custom-call | bytes 12000000 | tf_op jit(solution)/shard_map/inner_outputs/pallas_call | solution.py:289
  87.1 29.1 %all-to-all-done.2 = bf16[64,80,128]{2,1,0:T(8,128)(2,1)} async-done(((bf16[64,80,128]{2,1,0:T(8,128)(2,1)}), bf16[64,80,128]{2,1,0:T(8,128)(2,1)}, u32[]{:S(2)}, u32[]{:S(2)}) %all-to-all-start.2) | async-done | bytes 1310752 | tf_op jit(solution)/shard_map/all_to_all | solution.py:287
  116.1 3.3 %outputs.1 = bf16[128,5120]{1,0:T(8,128)(2,1)} custom-call(f32[128,5120]{1,0:T(8,128)S(1)} %inner_outputs.1.part_ref, bf16[80,128]{1,0:T(8,128)(2,1)S(1)} %bitcast.8, bf16[128,128]{1,0:T(8,128)(2,1)S(1)} %copy-done.3, bf16[8,8,80,128]{3,2,1,0:T(8,128)(2,1)} %bitcast.4.h_ref), custom_call_target="tpu_custom_call" | custom-call | tf_op jit(solution)/shard_map/outputs/pallas_call | solution.py:300
  (2 shorter events, 0.0 us)
Async XLA Ops:
  53.5 19.0 %all-to-all-start.1 = ((bf16[8,88,128]{2,1,0:T(8,128)(2,1)}), bf16[8,88,128]{2,1,0:T(8,128)(2,1)S(1)}, u32[]{:S(2)}, u32[]{:S(2)}) async-start(bf16[8,88,128]{2,1,0:T(8,128)(2,1)} %block_total.1), calls=%async_computation.1 | async-start | bytes 360448 | tf_op jit(solution)/shard_map/all_to_all | solution.py:272
  74.1 8.5 %copy-start.5 = (f32[80]{0:T(128)S(1)}, f32[80]{0:T(128)}, u32[]{:S(2)}) copy-start(f32[80]{0:T(128)} %param.11) | copy-start | bytes 964
  74.1 8.5 %copy-start.1 = (bf16[128,80]{0,1:T(8,128)(2,1)S(1)}, bf16[128,80]{0,1:T(8,128)(2,1)}, u32[]{:S(2)}) copy-start(bf16[128,80]{0,1:T(8,128)(2,1)} %param.8) | copy-start | bytes 61444
  74.1 8.5 %copy-start.2 = (bf16[128,128]{1,0:T(8,128)(2,1)S(1)}, bf16[128,128]{1,0:T(8,128)(2,1)}, u32[]{:S(2)}) copy-start(bf16[128,128]{1,0:T(8,128)(2,1)} %in_ref.3) | copy-start | bytes 98308
  74.1 8.5 %copy-start.3 = (bf16[128,128]{1,0:T(8,128)(2,1)S(1)}, bf16[128,128]{1,0:T(8,128)(2,1)}, u32[]{:S(2)}) copy-start(bf16[128,128]{1,0:T(8,128)(2,1)} %map_ref.3) | copy-start | bytes 98308
  74.1 8.5 %copy-start.4 = (bf16[128,80]{0,1:T(8,128)(2,1)S(1)}, bf16[128,80]{0,1:T(8,128)(2,1)}, u32[]{:S(2)}) copy-start(bf16[128,80]{0,1:T(8,128)(2,1)} %param.7) | copy-start | bytes 61444
  74.2 42.0 %all-to-all-start.2 = ((bf16[64,80,128]{2,1,0:T(8,128)(2,1)}), bf16[64,80,128]{2,1,0:T(8,128)(2,1)}, u32[]{:S(2)}, u32[]{:S(2)}) async-start(bf16[64,80,128]{2,1,0:T(8,128)(2,1)} %entering_states.1), calls=%async_computation.2 | async-start | bytes 2621440 | tf_op jit(solution)/shard_map/all_to_all | solution.py:287
  82.6 1.3 %copy-start = (bf16[128,5120]{1,0:T(8,128)(2,1)S(1)}, bf16[128,5120]{1,0:T(8,128)(2,1)}, u32[]{:S(2)}) copy-start(bf16[128,5120]{1,0:T(8,128)(2,1)} %x_ref.3) | copy-start | bytes 3932164

commit v3 on v2

--- a/solution.py
+++ b/solution.py
@@ -143,7 +143,7 @@
         out_ref[z, ROWS_H:ROWS_S, :] = sums
 
 
-def enter_kernel(s_ref, u_ref, z_ref, out_ref, dec_ref, udec_ref, out_buf, sems):
+def enter_kernel(s_ref, u_ref, z_ref, _, out_ref, dec_ref, udec_ref):
     decays(s_ref, dec_ref)
     decays(u_ref, udec_ref)
     mine = z_ref[0]
@@ -152,24 +152,15 @@
         later = follow(state, u_ref, z, udec_ref, z)
         state = tuple(jnp.where(z < mine, new, old) for new, old in zip(later, state))
 
-    def store(g):
-        return pltpu.make_async_copy(out_buf.at[pl.ds(g * NB, NB)], out_ref.at[pl.ds(g * NB, NB)], sems.at[g])
-
-    def group(g, state):
-        for i in range(NB):
-            c = g * NB + i
-            for j in range(TILES):
-                out_buf[c, j * ROWS:(j + 1) * ROWS, :] = state[j].astype(bf16)
-            state = follow(state, s_ref, c, dec_ref, c)
-        store(g).start()
-        return state
-
-    lax.fori_loop(0, GROUP // NB, group, state)
-    for g in range(GROUP // NB):
-        store(g).wait()
-
-
-def inner_kernel(x_ref, dt_ref, rate_ref, in_ref, map_ref, gain_ref, out_ref, b_ref, a_ref, g_ref, oh_ref):
+    def step(c, state):
+        for j in range(TILES):
+            out_ref[c, j * ROWS:(j + 1) * ROWS, :] = state[j].astype(bf16)
+        return follow(state, s_ref, c, dec_ref, c)
+
+    lax.fori_loop(0, GROUP, step, state, unroll=8)
+
+
+def inner_kernel(x_ref, dt_ref, rate_ref, in_ref, map_ref, gain_ref, out_ref, decay_ref, b_ref, a_ref, g_ref, oh_ref):
     g = pl.program_id(0)
 
     @pl.when(g == 0)
@@ -178,6 +169,7 @@
         mid = c[TOK // 2 - 1:TOK // 2, :]
         b_ref[...] = jnp.exp(c - mid) * dt
         a_ref[...] = jnp.exp(mid - c)
+        decay_ref[...] = jnp.exp(-c)
         score = lax.dot_general(map_ref[...], in_ref[...], (((1,), (1,)), ((), ())), preferred_element_type=f32)
         g_ref[...] = jnp.where(iota((TOK, TOK), 0) >= iota((TOK, TOK), 1), score, 0.0).astype(bf16)
         oh_ref[...] = one_hot()
@@ -193,29 +185,22 @@
         out_ref[:, cols] = gain * x + weight * dot(g_ref[...], xs)
 
 
-def output_kernel(part_ref, rate_ref, map_ref, h_ref, out_ref, h_buf, out_buf, h_sems, out_sems, weight_buf):
-    def load(b):
-        return pltpu.make_async_copy(h_ref.at[:, b], h_buf.at[b], h_sems.at[b])
-
+def output_kernel(part_ref, decay_ref, map_ref, h_ref, out_ref, out_buf, out_sems):
     def store(b):
         return pltpu.make_async_copy(out_buf.at[b], out_ref.at[:, columns(b)], out_sems.at[b])
 
-    for b in range(NB):
-        load(b).start()
-    decay = jnp.exp(-across(triangle(), rate_ref[...]))
+    decay = decay_ref[...]
     oh = one_hot()
     for b in range(NB):
-        weight_buf[b] = dot(split2(pltpu.roll(decay, (128 - HB * b) % 128, 1)), oh)
-    for b in range(NB):
-        load(b).wait()
         entering = jnp.concatenate(
             [
-                jnp.concatenate([h_buf[b, a, j * ROWS:(j + 1) * ROWS, :] for a in range(NA)], axis=0)
+                jnp.concatenate([h_ref[a, b, j * ROWS:(j + 1) * ROWS, :] for a in range(NA)], axis=0)
                 for j in range(TILES)
             ],
             axis=1,
         )
-        carried = weight_buf[b] * dot(map_ref[...], entering)
+        weight = dot(split2(pltpu.roll(decay, (128 - HB * b) % 128, 1)), oh)
+        carried = weight * dot(map_ref[...], entering)
         out_buf[b] = (part_ref[:, columns(b)] + carried).astype(bf16)
         store(b).start()
     for b in range(NB):
@@ -264,54 +249,49 @@
     states = exchange(sent.reshape(GROUP, ROWS_S, 128), axis_index_groups=near)
     totals = pl.pallas_call(
         total_kernel,
-        out_shape=jax.ShapeDtypeStruct((nz, ROWS_S, 128), bf16),
+        out_shape=pltpu.VMEM((nz, ROWS_S, 128), bf16),
         scratch_shapes=[pltpu.VMEM((GROUP * DEC, COLS), f32)],
         compiler_params=params(),
         name="block_total",
     )(states)
     totals = exchange(totals, axis_index_groups=far)
-    entering = pl.pallas_call(
-        enter_kernel,
-        in_specs=[vmem, vmem, pl.BlockSpec(memory_space=pltpu.SMEM)],
-        out_specs=hbm,
-        out_shape=jax.ShapeDtypeStruct((GROUP, ROWS_H, 128), bf16),
-        scratch_shapes=[
-            pltpu.VMEM((GROUP * DEC, COLS), f32),
-            pltpu.VMEM((nz * DEC, COLS), f32),
-            pltpu.VMEM((GROUP, ROWS_H, 128), bf16),
-            pltpu.SemaphoreType.DMA((GROUP // NB,)),
-        ],
-        compiler_params=params(),
-        name="entering_states",
-    )(states, totals, (lax.axis_index("d") // GROUP).astype(jnp.int32).reshape(1))
-    entering = exchange(entering, axis_index_groups=near).reshape(NA, NB, ROWS_H, 128)
     gains = jnp.broadcast_to(jnp.pad(gain, (0, 128 - HEADS))[None, :], (8, 128))
-    part = pl.pallas_call(
+    part, decay = pl.pallas_call(
         inner_kernel,
         grid=(STEPS,),
         in_specs=[xspec] + small + [whole((TOK, STATE)), whole((8, 128))],
-        out_specs=xspec,
-        out_shape=jax.ShapeDtypeStruct(x.shape, f32),
+        out_specs=[xspec, whole((TOK, 128))],
+        out_shape=[pltpu.HBM(x.shape, f32), jax.ShapeDtypeStruct((TOK, 128), f32)],
         scratch_shapes=[matrix, matrix, pltpu.VMEM((TOK, TOK), bf16), hot],
         compiler_params=params(),
         cost_estimate=cost(4),
         name="inner_outputs",
     )(x, dt, rate, in_map, out_map, gains)
+    entering = pl.pallas_call(
+        enter_kernel,
+        in_specs=[vmem, vmem, pl.BlockSpec(memory_space=pltpu.SMEM), hbm],
+        out_specs=vmem,
+        out_shape=pltpu.VMEM((GROUP, ROWS_H, 128), bf16),
+        scratch_shapes=[
+            pltpu.VMEM((GROUP * DEC, COLS), f32),
+            pltpu.VMEM((nz * DEC, COLS), f32),
+        ],
+        compiler_params=params(),
+        name="entering_states",
+    )(states, totals, (lax.axis_index("d") // GROUP).astype(jnp.int32).reshape(1), decay)
+    entering = exchange(entering, axis_index_groups=near).reshape(NA, NB, ROWS_H, 128)
     return pl.pallas_call(
         output_kernel,
-        in_specs=[vmem, vmem, vmem, hbm],
+        in_specs=[vmem, vmem, vmem, vmem],
         out_specs=hbm,
         out_shape=jax.ShapeDtypeStruct(x.shape, bf16),
         scratch_shapes=[
-            pltpu.VMEM((NB, NA, ROWS_H, 128), bf16),
             pltpu.VMEM((NB, TOK, COLS), bf16),
             sems,
-            sems,
-            pltpu.VMEM((NB, TOK, COLS), f32),
         ],
         compiler_params=params(),
         name="outputs",
-    )(part, rate, out_map, entering)
+    )(part, decay, out_map, entering)
 
 
 def solution(mesh):

time: 120 us -> 117 us (0.975)
  blocking collectives: 48.1 us -> 89.8 us
  waiting for transfers between devices: 38.1 us -> 4.87 us
  starting transfers between devices: 18.4 us -> 10 us
  Pallas kernels: 13.4 us -> 12 us
  local copies, waits for them, and re-layouts: 1.35 us -> 0.04 us
    all_to_all x0 -> x1, blocking collectives: none -> 41.7 us  [local(): exchange(entering, axis_index_groups=near).reshape(NA, NB, ROWS_H, 128)]
    all_to_all x1 -> x0, waiting for transfers between devices: 29.1 us -> none  [local(): exchange(entering, axis_index_groups=near).reshape(NA, NB, ROWS_H, 128)]
    all_to_all x1 -> x0, starting transfers between devices: 8.4 us -> none  [local(): exchange(entering, axis_index_groups=near).reshape(NA, NB, ROWS_H, 128)]
    all_to_all x1, waiting for transfers between devices: 9.01 us -> 4.87 us  [local(): totals = exchange(totals, axis_index_groups=far)]
    pallas_call x2, Pallas kernels: 4.86 us -> 3.28 us  [the longest x1 1.76 us: local(): pl.pallas_call(output_kernel, in_specs=[vmem, vmem, vmem, vmem], out_spec...]
    unnamed x12 -> x14, local copies, waits for them, and re-layouts: 1.34 us -> 0.03 us
  transfers between devices with their start and end apart: 2 -> 1, of which waited for: 2 -> 1; matrix products, arithmetic and copies ran while one was open for 0% -> 0% of each run, Pallas kernels for 3% -> 3%
where the time goes in v3:
time: 117 us
  blocking collectives  89.8 us (77%)
  Pallas kernels  12 us (10%)
  starting transfers between devices  10 us (9%)
  waiting for transfers between devices  4.87 us (4%)
    all_to_all x1, blocking collectives, local(): states = exchange(sent.reshape(GROUP, ROWS_S, 128), axis_index_groups=near)  48.1 us
    all_to_all x1, blocking collectives, local(): exchange(entering, axis_index_groups=near).reshape(NA, NB, ROWS_H, 128)  41.7 us
    all_to_all x1, starting transfers between devices, local(): totals = exchange(totals, axis_index_groups=far)  10 us
    all_to_all x1, waiting for transfers between devices, local(): totals = exchange(totals, axis_index_groups=far)  4.87 us
    pallas_call x1, Pallas kernels, local(): pl.pallas_call(inner_kernel, grid=(STEPS,), in_specs=[xspec] + small + [w...  4.04 us
    pallas_call x1, Pallas kernels, local(): pl.pallas_call(state_kernel, in_specs=[pl.BlockSpec(memory_space=pltpu.HB...  3.85 us
  transfers between devices with their start and end apart: 1, of which 1 were waited for; matrix products, arithmetic and copies ran while one was open for 0% of the time, Pallas kernels for 3%

profile of v3, /device:TPU:1, one launch (start us, length us, event | category | flops | bytes accessed | tf_op | source)
XLA Modules:
  0.0 116.8 jit_solution(4145995839581493954)
XLA Ops:
  0.0 3.8 %chunk_states.1 = bf16[8,8,88,128]{3,2,1,0:T(8,128)(2,1)S(1)} custom-call(bf16[128,5120]{1,0:T(8,128)(2,1)} %x_ref.3, bf16[80,128]{1,0:T(8,128)(2,1)} %bitcast.7, bf16[80,128]{1,0:T(8,128)(2,1)} %bitcast.9, bf16[128,128]{1,0:T(8,128)(2,1)} %in_ref.3), custom_call_target="tpu_custom_call" | custom-call | tf_op jit(solution)/shard_map/chunk_states/pallas_call | solution.py:235
  3.9 48.1 %all_to_all.15.s_ref = bf16[64,88,128]{2,1,0:T(8,128)(2,1)S(1)} all-to-all(bf16[64,88,128]{2,1,0:T(8,128)(2,1)S(1)} %bitcast.5), channel_id=1, replica_groups={{0,1,2,3,4,5,6,7,8,9,10,11,12,13,14,15,16,17,18,19,20,21,22,23,24,25,26..., dimensions={0} | all-to-all | bytes 2883584 | tf_op jit(solution)/shard_map/all_to_all | solution.py:249
  51.9 0.0 copy-start.6
  51.9 0.0 copy-start
  51.9 0.0 copy-start.2
  51.9 0.0 copy-start.3
  51.9 0.0 copy-start.4
  52.0 0.0 copy-start.5
  52.0 1.5 %block_total.1 = bf16[8,88,128]{2,1,0:T(8,128)(2,1)} custom-call(bf16[64,88,128]{2,1,0:T(8,128)(2,1)S(1)} %all_to_all.15.s_ref), custom_call_target="tpu_custom_call" | custom-call | tf_op jit(solution)/shard_map/block_total/pallas_call | solution.py:250
  53.5 10.0 %all-to-all-start.1 = ((bf16[8,88,128]{2,1,0:T(8,128)(2,1)}), bf16[8,88,128]{2,1,0:T(8,128)(2,1)S(1)}, u32[]{:S(2)}, u32[]{:S(2)}) async-start(bf16[8,88,128]{2,1,0:T(8,128)(2,1)} %block_total.1), calls=%async_computation.1 | async-start | bytes 360448 | tf_op jit(solution)/shard_map/all_to_all | solution.py:257
  63.5 0.0 copy-done.6
  63.5 0.0 copy-done
  63.6 0.0 copy-done.2
  63.6 0.0 copy-done.3
  63.6 0.0 copy-done.4
  63.6 0.0 copy-done.5
  63.6 4.0 %inner_outputs.1 = (f32[128,5120]{1,0:T(8,128)}, f32[128,128]{1,0:T(8,128)S(1)}) custom-call(bf16[128,5120]{1,0:T(8,128)(2,1)S(1)} %copy-done, bf16[80,128]{1,0:T(8,128)(2,1)S(1)} %bitcast.8, bf16[80,128]{1,0:T(8,128)(2,1)S(1)} %bitcast.10, bf16[128,128]{1,0:T(8,128)(2,1)S(1)} %copy-done.2, bf16[128,128]{1,0:T(8,128)(2,1)S(1)} %copy-done.3, ...), custom_call_target="tpu_custom_call" | custom-call | bytes 12000000 | tf_op jit(solution)/shard_map/inner_outputs/pallas_call | solution.py:259
  67.6 4.9 %all-to-all-done.1.u_ref = bf16[8,88,128]{2,1,0:T(8,128)(2,1)S(1)} async-done(((bf16[8,88,128]{2,1,0:T(8,128)(2,1)}), bf16[8,88,128]{2,1,0:T(8,128)(2,1)S(1)}, u32[]{:S(2)}, u32[]{:S(2)}) %all-to-all-start.1) | async-done | bytes 180256 | tf_op jit(solution)/shard_map/all_to_all | solution.py:257
  72.5 0.8 entering_states.1
  73.3 0.0 copy-start.1
  73.3 41.7 %all_to_all.16 = bf16[64,80,128]{2,1,0:T(8,128)(2,1)S(1)} all-to-all(bf16[64,80,128]{2,1,0:T(8,128)(2,1)S(1)} %entering_states.1), channel_id=1, replica_groups={{0,1,2,3,4,5,6,7,8,9,10,11,12,13,14,15,16,17,18,19,20,21,22,23,24,25,26..., dimensions={0} | all-to-all | bytes 2621440 | tf_op jit(solution)/shard_map/all_to_all | solution.py:282
  115.0 0.0 copy-done.1
  115.0 1.8 %outputs.1 = bf16[128,5120]{1,0:T(8,128)(2,1)} custom-call(f32[128,5120]{1,0:T(8,128)S(1)} %copy-done.1, f32[128,128]{1,0:T(8,128)S(1)} %get-tuple-element.8._.decay_ref, bf16[128,128]{1,0:T(8,128)(2,1)S(1)} %copy-done.3, bf16[8,8,80,128]{3,2,1,0:T(8,128)(2,1)S(1)} %bitcast.6), custom_call_target="tpu_custom_call" | custom-call | tf_op jit(solution)/shard_map/outputs/pallas_call | solution.py:283
  (2 shorter events, 0.0 us)
Async XLA Ops:
  51.9 11.6 %copy-start.6 = (f32[80]{0:T(128)S(1)}, f32[80]{0:T(128)}, u32[]{:S(2)}) copy-start(f32[80]{0:T(128)} %param.11) | copy-start | bytes 964
  51.9 11.6 %copy-start = (bf16[128,5120]{1,0:T(8,128)(2,1)S(1)}, bf16[128,5120]{1,0:T(8,128)(2,1)}, u32[]{:S(2)}) copy-start(bf16[128,5120]{1,0:T(8,128)(2,1)} %x_ref.3) | copy-start | bytes 3932164
  51.9 11.6 %copy-start.2 = (bf16[128,128]{1,0:T(8,128)(2,1)S(1)}, bf16[128,128]{1,0:T(8,128)(2,1)}, u32[]{:S(2)}) copy-start(bf16[128,128]{1,0:T(8,128)(2,1)} %in_ref.3) | copy-start | bytes 98308
  51.9 11.6 %copy-start.3 = (bf16[128,128]{1,0:T(8,128)(2,1)S(1)}, bf16[128,128]{1,0:T(8,128)(2,1)}, u32[]{:S(2)}) copy-start(bf16[128,128]{1,0:T(8,128)(2,1)} %map_ref.3) | copy-start | bytes 98308
  51.9 11.6 %copy-start.4 = (bf16[128,80]{0,1:T(8,128)(2,1)S(1)}, bf16[128,80]{0,1:T(8,128)(2,1)}, u32[]{:S(2)}) copy-start(bf16[128,80]{0,1:T(8,128)(2,1)} %param.7) | copy-start | bytes 61444
  52.0 11.6 %copy-start.5 = (bf16[128,80]{0,1:T(8,128)(2,1)S(1)}, bf16[128,80]{0,1:T(8,128)(2,1)}, u32[]{:S(2)}) copy-start(bf16[128,80]{0,1:T(8,128)(2,1)} %param.8) | copy-start | bytes 61444
  53.5 19.0 %all-to-all-start.1 = ((bf16[8,88,128]{2,1,0:T(8,128)(2,1)}), bf16[8,88,128]{2,1,0:T(8,128)(2,1)S(1)}, u32[]{:S(2)}, u32[]{:S(2)}) async-start(bf16[8,88,128]{2,1,0:T(8,128)(2,1)} %block_total.1), calls=%async_computation.1 | async-start | bytes 360448 | tf_op jit(solution)/shard_map/all_to_all | solution.py:257
  73.3 41.7 %copy-start.1 = (f32[128,5120]{1,0:T(8,128)S(1)}, f32[128,5120]{1,0:T(8,128)}, u32[]{:S(2)}) copy-start(f32[128,5120]{1,0:T(8,128)} %get-tuple-element.7.part_ref) | copy-start | bytes 7864324

commit v4 on v3

--- a/solution.py
+++ b/solution.py
@@ -84,7 +84,8 @@
     lane = iota((8, 128), 1)
     for b in range(NB):
         sums = pieces(pltpu.roll(total, (128 - HB * b) % 128, 1), lane)
-        load(b).wait()
+        for i in {0: range(3), 3: range(3, NB)}.get(b, ()):
+            load(i).wait()
         for j in range(TILES):
             h = b * HB + 2 * j
             rows = jnp.concatenate([bt_ref[...] * w_ref[h:h + 1, :], bt_ref[...] * w_ref[h + 1:h + 2, :]], axis=0)

time: 117 us -> 116 us (level)
  no operation moved by 1% of the time
where the time goes in v4:
time: 116 us
  blocking collectives  89.7 us (77%)
  Pallas kernels  11.1 us (10%)
  starting transfers between devices  10 us (9%)
  waiting for transfers between devices  4.89 us (4%)
    all_to_all x1, blocking collectives, local(): states = exchange(sent.reshape(GROUP, ROWS_S, 128), axis_index_groups=near)  48.1 us
    all_to_all x1, blocking collectives, local(): exchange(entering, axis_index_groups=near).reshape(NA, NB, ROWS_H, 128)  41.7 us
    all_to_all x1, starting transfers between devices, local(): totals = exchange(totals, axis_index_groups=far)  10 us
    all_to_all x1, waiting for transfers between devices, local(): totals = exchange(totals, axis_index_groups=far)  4.89 us
    pallas_call x1, Pallas kernels, local(): pl.pallas_call(inner_kernel, grid=(STEPS,), in_specs=[xspec] + small + [w...  4.04 us
    pallas_call x1, Pallas kernels, local(): pl.pallas_call(state_kernel, in_specs=[pl.BlockSpec(memory_space=pltpu.HB...  2.97 us
  transfers between devices with their start and end apart: 1, of which 1 were waited for; matrix products, arithmetic and copies ran while one was open for 0% of the time, Pallas kernels for 3%

profile of v4, /device:TPU:1, one launch (start us, length us, event | category | flops | bytes accessed | tf_op | source)
XLA Modules:
  0.0 115.9 jit_solution(10562740918159494675)
XLA Ops:
  0.0 3.0 %chunk_states.1 = bf16[8,8,88,128]{3,2,1,0:T(8,128)(2,1)S(1)} custom-call(bf16[128,5120]{1,0:T(8,128)(2,1)} %x_ref.3, bf16[80,128]{1,0:T(8,128)(2,1)} %bitcast.7, bf16[80,128]{1,0:T(8,128)(2,1)} %bitcast.9, bf16[128,128]{1,0:T(8,128)(2,1)} %in_ref.3), custom_call_target="tpu_custom_call" | custom-call | tf_op jit(solution)/shard_map/chunk_states/pallas_call | solution.py:236
  3.0 48.1 %all_to_all.15.s_ref = bf16[64,88,128]{2,1,0:T(8,128)(2,1)S(1)} all-to-all(bf16[64,88,128]{2,1,0:T(8,128)(2,1)S(1)} %bitcast.5), channel_id=1, replica_groups={{0,1,2,3,4,5,6,7,8,9,10,11,12,13,14,15,16,17,18,19,20,21,22,23,24,25,26..., dimensions={0} | all-to-all | bytes 2883584 | tf_op jit(solution)/shard_map/all_to_all | solution.py:250
  51.1 0.0 copy-start.6
  51.1 0.0 copy-start
  51.1 0.0 copy-start.2
  51.1 0.0 copy-start.3
  51.1 0.0 copy-start.4
  51.1 0.0 copy-start.5
  51.1 1.5 %block_total.1 = bf16[8,88,128]{2,1,0:T(8,128)(2,1)} custom-call(bf16[64,88,128]{2,1,0:T(8,128)(2,1)S(1)} %all_to_all.15.s_ref), custom_call_target="tpu_custom_call" | custom-call | tf_op jit(solution)/shard_map/block_total/pallas_call | solution.py:251
  52.6 10.0 %all-to-all-start.1 = ((bf16[8,88,128]{2,1,0:T(8,128)(2,1)}), bf16[8,88,128]{2,1,0:T(8,128)(2,1)S(1)}, u32[]{:S(2)}, u32[]{:S(2)}) async-start(bf16[8,88,128]{2,1,0:T(8,128)(2,1)} %block_total.1), calls=%async_computation.1 | async-start | bytes 360448 | tf_op jit(solution)/shard_map/all_to_all | solution.py:258
  62.6 0.0 copy-done.6
  62.7 0.0 copy-done
  62.7 0.0 copy-done.2
  62.7 0.0 copy-done.3
  62.7 0.0 copy-done.4
  62.7 0.0 copy-done.5
  62.7 4.0 %inner_outputs.1 = (f32[128,5120]{1,0:T(8,128)}, f32[128,128]{1,0:T(8,128)S(1)}) custom-call(bf16[128,5120]{1,0:T(8,128)(2,1)S(1)} %copy-done, bf16[80,128]{1,0:T(8,128)(2,1)S(1)} %bitcast.8, bf16[80,128]{1,0:T(8,128)(2,1)S(1)} %bitcast.10, bf16[128,128]{1,0:T(8,128)(2,1)S(1)} %copy-done.2, bf16[128,128]{1,0:T(8,128)(2,1)S(1)} %copy-done.3, ...), custom_call_target="tpu_custom_call" | custom-call | bytes 12000000 | tf_op jit(solution)/shard_map/inner_outputs/pallas_call | solution.py:260
  66.8 4.9 %all-to-all-done.1.u_ref = bf16[8,88,128]{2,1,0:T(8,128)(2,1)S(1)} async-done(((bf16[8,88,128]{2,1,0:T(8,128)(2,1)}), bf16[8,88,128]{2,1,0:T(8,128)(2,1)S(1)}, u32[]{:S(2)}, u32[]{:S(2)}) %all-to-all-start.1) | async-done | bytes 180256 | tf_op jit(solution)/shard_map/all_to_all | solution.py:258
  71.6 0.8 entering_states.1
  72.4 0.0 copy-start.1
  72.4 41.7 %all_to_all.16 = bf16[64,80,128]{2,1,0:T(8,128)(2,1)S(1)} all-to-all(bf16[64,80,128]{2,1,0:T(8,128)(2,1)S(1)} %entering_states.1), channel_id=1, replica_groups={{0,1,2,3,4,5,6,7,8,9,10,11,12,13,14,15,16,17,18,19,20,21,22,23,24,25,26..., dimensions={0} | all-to-all | bytes 2621440 | tf_op jit(solution)/shard_map/all_to_all | solution.py:283
  114.1 0.0 copy-done.1
  114.1 1.8 %outputs.1 = bf16[128,5120]{1,0:T(8,128)(2,1)} custom-call(f32[128,5120]{1,0:T(8,128)S(1)} %copy-done.1, f32[128,128]{1,0:T(8,128)S(1)} %get-tuple-element.8._.decay_ref, bf16[128,128]{1,0:T(8,128)(2,1)S(1)} %copy-done.3, bf16[8,8,80,128]{3,2,1,0:T(8,128)(2,1)S(1)} %bitcast.6), custom_call_target="tpu_custom_call" | custom-call | tf_op jit(solution)/shard_map/outputs/pallas_call | solution.py:284
  (2 shorter events, 0.0 us)
Async XLA Ops:
  51.1 11.6 %copy-start.6 = (f32[80]{0:T(128)S(1)}, f32[80]{0:T(128)}, u32[]{:S(2)}) copy-start(f32[80]{0:T(128)} %param.11) | copy-start | bytes 964
  51.1 11.6 %copy-start = (bf16[128,5120]{1,0:T(8,128)(2,1)S(1)}, bf16[128,5120]{1,0:T(8,128)(2,1)}, u32[]{:S(2)}) copy-start(bf16[128,5120]{1,0:T(8,128)(2,1)} %x_ref.3) | copy-start | bytes 3932164
  51.1 11.6 %copy-start.2 = (bf16[128,128]{1,0:T(8,128)(2,1)S(1)}, bf16[128,128]{1,0:T(8,128)(2,1)}, u32[]{:S(2)}) copy-start(bf16[128,128]{1,0:T(8,128)(2,1)} %in_ref.3) | copy-start | bytes 98308
  51.1 11.6 %copy-start.3 = (bf16[128,128]{1,0:T(8,128)(2,1)S(1)}, bf16[128,128]{1,0:T(8,128)(2,1)}, u32[]{:S(2)}) copy-start(bf16[128,128]{1,0:T(8,128)(2,1)} %map_ref.3) | copy-start | bytes 98308
  51.1 11.6 %copy-start.4 = (bf16[128,80]{0,1:T(8,128)(2,1)S(1)}, bf16[128,80]{0,1:T(8,128)(2,1)}, u32[]{:S(2)}) copy-start(bf16[128,80]{0,1:T(8,128)(2,1)} %param.7) | copy-start | bytes 61444
  51.1 11.6 %copy-start.5 = (bf16[128,80]{0,1:T(8,128)(2,1)S(1)}, bf16[128,80]{0,1:T(8,128)(2,1)}, u32[]{:S(2)}) copy-start(bf16[128,80]{0,1:T(8,128)(2,1)} %param.8) | copy-start | bytes 61444
  52.6 19.0 %all-to-all-start.1 = ((bf16[8,88,128]{2,1,0:T(8,128)(2,1)}), bf16[8,88,128]{2,1,0:T(8,128)(2,1)S(1)}, u32[]{:S(2)}, u32[]{:S(2)}) async-start(bf16[8,88,128]{2,1,0:T(8,128)(2,1)} %block_total.1), calls=%async_computation.1 | async-start | bytes 360448 | tf_op jit(solution)/shard_map/all_to_all | solution.py:258
  72.4 41.7 %copy-start.1 = (f32[128,5120]{1,0:T(8,128)S(1)}, f32[128,5120]{1,0:T(8,128)}, u32[]{:S(2)}) copy-start(f32[128,5120]{1,0:T(8,128)} %get-tuple-element.7.part_ref) | copy-start | bytes 7864324

commit v5 on v3

--- a/solution.py
+++ b/solution.py
@@ -67,12 +67,20 @@
     return slice(b * COLS, (b + 1) * COLS)
 
 
-def state_kernel(x_ref, dt_ref, rate_ref, in_ref, out_ref, x_buf, x_sems, w_ref, bt_ref):
+def state_kernel(x_ref, dt_hbm, rate_hbm, in_hbm, out_ref, x_buf, x_sems, w_ref, bt_ref, dt_ref, rate_ref, in_ref, sems):
     def load(b):
         return pltpu.make_async_copy(x_ref.at[:, columns(b)], x_buf.at[b], x_sems.at[b])
 
+    small = [
+        pltpu.make_async_copy(src, dst, sems.at[i])
+        for i, (src, dst) in enumerate([(rate_hbm, rate_ref), (dt_hbm, dt_ref), (in_hbm, in_ref)])
+    ]
+    for copy in small:
+        copy.start()
     for b in range(NB):
         load(b).start()
+    for copy in small:
+        copy.wait()
     rate = rate_ref[...]
     c = dot(rate, triangle(upper=True))
     w_ref[...] = jnp.exp(c - c[:, TOK - 1:TOK]) * dt_ref[...].astype(f32)
@@ -83,8 +91,9 @@
     left = iota((STATE, 128), 1) < HEAD_DIM
     lane = iota((8, 128), 1)
     for b in range(NB):
+        load(b).wait()
+    for b in range(NB):
         sums = pieces(pltpu.roll(total, (128 - HB * b) % 128, 1), lane)
-        load(b).wait()
         for j in range(TILES):
             h = b * HB + 2 * j
             rows = jnp.concatenate([bt_ref[...] * w_ref[h:h + 1, :], bt_ref[...] * w_ref[h + 1:h + 2, :]], axis=0)
@@ -234,7 +243,7 @@
     sems = pltpu.SemaphoreType.DMA((NB,))
     sent = pl.pallas_call(
         state_kernel,
-        in_specs=[pl.BlockSpec(memory_space=pltpu.HBM), vmem, vmem, vmem],
+        in_specs=[pl.BlockSpec(memory_space=pltpu.HBM)] * 4,
         out_specs=vmem,
         out_shape=pltpu.VMEM((NA, NB, ROWS_S, 128), bf16),
         scratch_shapes=[
@@ -242,6 +251,10 @@
             sems,
             pltpu.VMEM((HEADS, TOK), f32),
             pltpu.VMEM((STATE, TOK), f32),
+            pltpu.VMEM((HEADS, TOK), bf16),
+            pltpu.VMEM((HEADS, TOK), bf16),
+            pltpu.VMEM((TOK, STATE), bf16),
+            pltpu.SemaphoreType.DMA((3,)),
         ],
         compiler_params=pltpu.CompilerParams(vmem_limit_bytes=56 << 20),
         name="chunk_states",

time: 117 us -> 116 us (level)
  Pallas kernels: 12 us -> 10.6 us
    pallas_call x1, Pallas kernels: 3.85 us -> 2.47 us  [local(): pl.pallas_call(state_kernel, in_specs=[pl.BlockSpec(memory_space=pltpu.HB...]
  transfers between devices with their start and end apart: 1 -> 1, of which waited for: 1 -> 1; matrix products, arithmetic and copies ran while one was open for 0% -> 0% of each run, Pallas kernels for 3% -> 4%
where the time goes in v5:
time: 116 us; the launch traced here: 115 us
  blocking collectives  89.7 us (77%)
  Pallas kernels  10.6 us (9%)
  starting transfers between devices  10 us (9%)
  waiting for transfers between devices  4.86 us (4%)
    all_to_all x1, blocking collectives, local(): states = exchange(sent.reshape(GROUP, ROWS_S, 128), axis_index_groups=near)  48.1 us
    all_to_all x1, blocking collectives, local(): exchange(entering, axis_index_groups=near).reshape(NA, NB, ROWS_H, 128)  41.7 us
    all_to_all x1, starting transfers between devices, local(): totals = exchange(totals, axis_index_groups=far)  10 us
    all_to_all x1, waiting for transfers between devices, local(): totals = exchange(totals, axis_index_groups=far)  4.86 us
    pallas_call x1, Pallas kernels, local(): pl.pallas_call(inner_kernel, grid=(STEPS,), in_specs=[xspec] + small + [w...  4.05 us
    pallas_call x1, Pallas kernels, local(): pl.pallas_call(state_kernel, in_specs=[pl.BlockSpec(memory_space=pltpu.HB...  2.47 us
  transfers between devices with their start and end apart: 1, of which 1 were waited for; matrix products, arithmetic and copies ran while one was open for 0% of the time, Pallas kernels for 4%

profile of v5, /device:TPU:1, one launch (start us, length us, event | category | flops | bytes accessed | tf_op | source)
XLA Modules:
  0.0 115.4 jit_solution(754781119265208947)
XLA Ops:
  0.0 2.5 %chunk_states.1 = bf16[8,8,88,128]{3,2,1,0:T(8,128)(2,1)S(1)} custom-call(bf16[128,5120]{1,0:T(8,128)(2,1)} %x_ref.3, bf16[80,128]{1,0:T(8,128)(2,1)} %bitcast.7, bf16[80,128]{1,0:T(8,128)(2,1)} %bitcast.9, bf16[128,128]{1,0:T(8,128)(2,1)} %in_hbm.1), custom_call_target="tpu_custom_call" | custom-call | tf_op jit(solution)/shard_map/chunk_states/pallas_call | solution.py:244
  2.5 48.1 %all_to_all.15.s_ref = bf16[64,88,128]{2,1,0:T(8,128)(2,1)S(1)} all-to-all(bf16[64,88,128]{2,1,0:T(8,128)(2,1)S(1)} %bitcast.5), channel_id=1, replica_groups={{0,1,2,3,4,5,6,7,8,9,10,11,12,13,14,15,16,17,18,19,20,21,22,23,24,25,26..., dimensions={0} | all-to-all | bytes 2883584 | tf_op jit(solution)/shard_map/all_to_all | solution.py:262
  50.6 0.0 copy-start.6
  50.6 0.0 copy-start
  50.6 0.0 copy-start.2
  50.6 0.0 copy-start.3
  50.6 0.0 copy-start.4
  50.6 0.0 copy-start.5
  50.6 1.5 %block_total.1 = bf16[8,88,128]{2,1,0:T(8,128)(2,1)} custom-call(bf16[64,88,128]{2,1,0:T(8,128)(2,1)S(1)} %all_to_all.15.s_ref), custom_call_target="tpu_custom_call" | custom-call | tf_op jit(solution)/shard_map/block_total/pallas_call | solution.py:263
  52.1 10.0 %all-to-all-start.1 = ((bf16[8,88,128]{2,1,0:T(8,128)(2,1)}), bf16[8,88,128]{2,1,0:T(8,128)(2,1)S(1)}, u32[]{:S(2)}, u32[]{:S(2)}) async-start(bf16[8,88,128]{2,1,0:T(8,128)(2,1)} %block_total.1), calls=%async_computation.1 | async-start | bytes 360448 | tf_op jit(solution)/shard_map/all_to_all | solution.py:270
  62.1 0.0 copy-done.6
  62.2 0.0 copy-done
  62.2 0.0 copy-done.2
  62.2 0.0 copy-done.3
  62.2 0.0 copy-done.4
  62.2 0.0 copy-done.5
  62.2 4.1 %inner_outputs.1 = (f32[128,5120]{1,0:T(8,128)}, f32[128,128]{1,0:T(8,128)S(1)}) custom-call(bf16[128,5120]{1,0:T(8,128)(2,1)S(1)} %copy-done, bf16[80,128]{1,0:T(8,128)(2,1)S(1)} %bitcast.8, bf16[80,128]{1,0:T(8,128)(2,1)S(1)} %bitcast.10, bf16[128,128]{1,0:T(8,128)(2,1)S(1)} %copy-done.2, bf16[128,128]{1,0:T(8,128)(2,1)S(1)} %copy-done.3, ...), custom_call_target="tpu_custom_call" | custom-call | bytes 12000000 | tf_op jit(solution)/shard_map/inner_outputs/pallas_call | solution.py:272
  66.3 4.9 %all-to-all-done.1.u_ref = bf16[8,88,128]{2,1,0:T(8,128)(2,1)S(1)} async-done(((bf16[8,88,128]{2,1,0:T(8,128)(2,1)}), bf16[8,88,128]{2,1,0:T(8,128)(2,1)S(1)}, u32[]{:S(2)}, u32[]{:S(2)}) %all-to-all-start.1) | async-done | bytes 180256 | tf_op jit(solution)/shard_map/all_to_all | solution.py:270
  71.1 0.8 entering_states.1
  71.9 0.0 copy-start.1
  71.9 41.7 %all_to_all.16 = bf16[64,80,128]{2,1,0:T(8,128)(2,1)S(1)} all-to-all(bf16[64,80,128]{2,1,0:T(8,128)(2,1)S(1)} %entering_states.1), channel_id=1, replica_groups={{0,1,2,3,4,5,6,7,8,9,10,11,12,13,14,15,16,17,18,19,20,21,22,23,24,25,26..., dimensions={0} | all-to-all | bytes 2621440 | tf_op jit(solution)/shard_map/all_to_all | solution.py:295
  113.6 0.0 copy-done.1
  113.6 1.8 %outputs.1 = bf16[128,5120]{1,0:T(8,128)(2,1)} custom-call(f32[128,5120]{1,0:T(8,128)S(1)} %copy-done.1, f32[128,128]{1,0:T(8,128)S(1)} %get-tuple-element.8._.decay_ref, bf16[128,128]{1,0:T(8,128)(2,1)S(1)} %copy-done.3, bf16[8,8,80,128]{3,2,1,0:T(8,128)(2,1)S(1)} %bitcast.6), custom_call_target="tpu_custom_call" | custom-call | tf_op jit(solution)/shard_map/outputs/pallas_call | solution.py:296
  (2 shorter events, 0.0 us)
Async XLA Ops:
  50.6 11.6 %copy-start.6 = (f32[80]{0:T(128)S(1)}, f32[80]{0:T(128)}, u32[]{:S(2)}) copy-start(f32[80]{0:T(128)} %param.11) | copy-start | bytes 964
  50.6 11.6 %copy-start = (bf16[128,5120]{1,0:T(8,128)(2,1)S(1)}, bf16[128,5120]{1,0:T(8,128)(2,1)}, u32[]{:S(2)}) copy-start(bf16[128,5120]{1,0:T(8,128)(2,1)} %x_ref.3) | copy-start | bytes 3932164
  50.6 11.6 %copy-start.2 = (bf16[128,128]{1,0:T(8,128)(2,1)S(1)}, bf16[128,128]{1,0:T(8,128)(2,1)}, u32[]{:S(2)}) copy-start(bf16[128,128]{1,0:T(8,128)(2,1)} %in_hbm.1) | copy-start | bytes 98308
  50.6 11.6 %copy-start.3 = (bf16[128,128]{1,0:T(8,128)(2,1)S(1)}, bf16[128,128]{1,0:T(8,128)(2,1)}, u32[]{:S(2)}) copy-start(bf16[128,128]{1,0:T(8,128)(2,1)} %map_ref.3) | copy-start | bytes 98308
  50.6 11.6 %copy-start.4 = (bf16[128,80]{0,1:T(8,128)(2,1)S(1)}, bf16[128,80]{0,1:T(8,128)(2,1)}, u32[]{:S(2)}) copy-start(bf16[128,80]{0,1:T(8,128)(2,1)} %param.7) | copy-start | bytes 61444
  50.6 11.6 %copy-start.5 = (bf16[128,80]{0,1:T(8,128)(2,1)S(1)}, bf16[128,80]{0,1:T(8,128)(2,1)}, u32[]{:S(2)}) copy-start(bf16[128,80]{0,1:T(8,128)(2,1)} %param.8) | copy-start | bytes 61444
  52.1 19.0 %all-to-all-start.1 = ((bf16[8,88,128]{2,1,0:T(8,128)(2,1)}), bf16[8,88,128]{2,1,0:T(8,128)(2,1)S(1)}, u32[]{:S(2)}, u32[]{:S(2)}) async-start(bf16[8,88,128]{2,1,0:T(8,128)(2,1)} %block_total.1), calls=%async_computation.1 | async-start | bytes 360448 | tf_op jit(solution)/shard_map/all_to_all | solution.py:270
  71.9 41.7 %copy-start.1 = (f32[128,5120]{1,0:T(8,128)S(1)}, f32[128,5120]{1,0:T(8,128)}, u32[]{:S(2)}) copy-start(f32[128,5120]{1,0:T(8,128)} %get-tuple-element.7.part_ref) | copy-start | bytes 7864324

commit v6 on v5

--- a/solution.py
+++ b/solution.py
@@ -169,7 +169,7 @@
     lax.fori_loop(0, GROUP, step, state, unroll=8)
 
 
-def inner_kernel(x_ref, dt_ref, rate_ref, in_ref, map_ref, gain_ref, out_ref, decay_ref, b_ref, a_ref, g_ref, oh_ref):
+def inner_kernel(x_ref, dt_ref, rate_ref, in_ref, map_ref, gain_ref, out_ref, done_ref, b_ref, a_ref, e_ref, g_ref, oh_ref):
     g = pl.program_id(0)
 
     @pl.when(g == 0)
@@ -178,7 +178,8 @@
         mid = c[TOK // 2 - 1:TOK // 2, :]
         b_ref[...] = jnp.exp(c - mid) * dt
         a_ref[...] = jnp.exp(mid - c)
-        decay_ref[...] = jnp.exp(-c)
+        e_ref[...] = jnp.exp(-c)
+        done_ref[...] = jnp.exp(-c[TOK - 8:, :])
         score = lax.dot_general(map_ref[...], in_ref[...], (((1,), (1,)), ((), ())), preferred_element_type=f32)
         g_ref[...] = jnp.where(iota((TOK, TOK), 0) >= iota((TOK, TOK), 1), score, 0.0).astype(bf16)
         oh_ref[...] = one_hot()
@@ -191,15 +192,14 @@
         xs = (dot(split2(pltpu.roll(b_ref[...], back, 1)), oh) * x).astype(bf16)
         gain = dot(split2(pltpu.roll(gain_ref[...], back, 1)), oh)[0:1, :]
         weight = dot(split2(pltpu.roll(a_ref[...], back, 1)), oh)
-        out_ref[:, cols] = gain * x + weight * dot(g_ref[...], xs)
-
-
-def output_kernel(part_ref, decay_ref, map_ref, h_ref, out_ref, out_buf, out_sems):
+        out_ref[0, :, cols] = gain * x + weight * dot(g_ref[...], xs)
+        out_ref[1, :, cols] = dot(split2(pltpu.roll(e_ref[...], back, 1)), oh)
+
+
+def output_kernel(part_ref, map_ref, h_ref, out_ref, out_buf, out_sems):
     def store(b):
         return pltpu.make_async_copy(out_buf.at[b], out_ref.at[:, columns(b)], out_sems.at[b])
 
-    decay = decay_ref[...]
-    oh = one_hot()
     for b in range(NB):
         entering = jnp.concatenate(
             [
@@ -208,9 +208,8 @@
             ],
             axis=1,
         )
-        weight = dot(split2(pltpu.roll(decay, (128 - HB * b) % 128, 1)), oh)
-        carried = weight * dot(map_ref[...], entering)
-        out_buf[b] = (part_ref[:, columns(b)] + carried).astype(bf16)
+        carried = part_ref[1, :, columns(b)] * dot(map_ref[...], entering)
+        out_buf[b] = (part_ref[0, :, columns(b)] + carried).astype(bf16)
         store(b).start()
     for b in range(NB):
         store(b).wait()
@@ -269,13 +268,13 @@
     )(states)
     totals = exchange(totals, axis_index_groups=far)
     gains = jnp.broadcast_to(jnp.pad(gain, (0, 128 - HEADS))[None, :], (8, 128))
-    part, decay = pl.pallas_call(
+    part, done = pl.pallas_call(
         inner_kernel,
         grid=(STEPS,),
         in_specs=[xspec] + small + [whole((TOK, STATE)), whole((8, 128))],
-        out_specs=[xspec, whole((TOK, 128))],
-        out_shape=[pltpu.HBM(x.shape, f32), jax.ShapeDtypeStruct((TOK, 128), f32)],
-        scratch_shapes=[matrix, matrix, pltpu.VMEM((TOK, TOK), bf16), hot],
+        out_specs=[pl.BlockSpec((2, TOK, BPS * COLS), lambda g: (0, 0, g)), whole((8, 128))],
+        out_shape=[pltpu.HBM((2, *x.shape), f32), jax.ShapeDtypeStruct((8, 128), f32)],
+        scratch_shapes=[matrix, matrix, matrix, pltpu.VMEM((TOK, TOK), bf16), hot],
         compiler_params=params(),
         cost_estimate=cost(4),
         name="inner_outputs",
@@ -291,11 +290,11 @@
         ],
         compiler_params=params(),
         name="entering_states",
-    )(states, totals, (lax.axis_index("d") // GROUP).astype(jnp.int32).reshape(1), decay)
+    )(states, totals, (lax.axis_index("d") // GROUP).astype(jnp.int32).reshape(1), done)
     entering = exchange(entering, axis_index_groups=near).reshape(NA, NB, ROWS_H, 128)
     return pl.pallas_call(
         output_kernel,
-        in_specs=[vmem, vmem, vmem, vmem],
+        in_specs=[vmem, vmem, vmem],
         out_specs=hbm,
         out_shape=jax.ShapeDtypeStruct(x.shape, bf16),
         scratch_shapes=[
@@ -304,7 +303,7 @@
         ],
         compiler_params=params(),
         name="outputs",
-    )(part, decay, out_map, entering)
+    )(part, out_map, entering)
 
 
 def solution(mesh):

time: 116 us -> 115 us (level)
  no operation moved by 1% of the time
where the time goes in v6:
time: 115 us
  blocking collectives  89.7 us (78%)
  Pallas kernels  11 us (10%)
  starting transfers between devices  10 us (9%)
  waiting for transfers between devices  4.04 us (4%)
    all_to_all x1, blocking collectives, local(): states = exchange(sent.reshape(GROUP, ROWS_S, 128), axis_index_groups=near)  48.1 us
    all_to_all x1, blocking collectives, local(): exchange(entering, axis_index_groups=near).reshape(NA, NB, ROWS_H, 128)  41.7 us
    all_to_all x1, starting transfers between devices, local(): totals = exchange(totals, axis_index_groups=far)  10 us
    pallas_call x1, Pallas kernels, local(): pl.pallas_call(inner_kernel, grid=(STEPS,), in_specs=[xspec] + small + [w...  4.87 us
    all_to_all x1, waiting for transfers between devices, local(): totals = exchange(totals, axis_index_groups=far)  4.04 us
    pallas_call x1, Pallas kernels, local(): pl.pallas_call(state_kernel, in_specs=[pl.BlockSpec(memory_space=pltpu.HB...  2.47 us
  transfers between devices with their start and end apart: 1, of which 1 were waited for; matrix products, arithmetic and copies ran while one was open for 0% of the time, Pallas kernels for 4%

profile of v6, /device:TPU:1, one launch (start us, length us, event | category | flops | bytes accessed | tf_op | source)
XLA Modules:
  0.0 114.9 jit_solution(8779545243762007673)
XLA Ops:
  0.0 2.5 %chunk_states.1 = bf16[8,8,88,128]{3,2,1,0:T(8,128)(2,1)S(1)} custom-call(bf16[128,5120]{1,0:T(8,128)(2,1)} %x_ref.3, bf16[80,128]{1,0:T(8,128)(2,1)} %bitcast.7, bf16[80,128]{1,0:T(8,128)(2,1)} %bitcast.9, bf16[128,128]{1,0:T(8,128)(2,1)} %in_hbm.1), custom_call_target="tpu_custom_call" | custom-call | tf_op jit(solution)/shard_map/chunk_states/pallas_call | solution.py:243
  2.5 48.1 %all_to_all.15.s_ref = bf16[64,88,128]{2,1,0:T(8,128)(2,1)S(1)} all-to-all(bf16[64,88,128]{2,1,0:T(8,128)(2,1)S(1)} %bitcast.5), channel_id=1, replica_groups={{0,1,2,3,4,5,6,7,8,9,10,11,12,13,14,15,16,17,18,19,20,21,22,23,24,25,26..., dimensions={0} | all-to-all | bytes 2883584 | tf_op jit(solution)/shard_map/all_to_all | solution.py:261
  50.6 0.0 copy-start.6
  50.6 0.0 copy-start
  50.6 0.0 copy-start.2
  50.6 0.0 copy-start.3
  50.6 0.0 copy-start.4
  50.6 0.0 copy-start.5
  50.6 1.5 %block_total.1 = bf16[8,88,128]{2,1,0:T(8,128)(2,1)} custom-call(bf16[64,88,128]{2,1,0:T(8,128)(2,1)S(1)} %all_to_all.15.s_ref), custom_call_target="tpu_custom_call" | custom-call | tf_op jit(solution)/shard_map/block_total/pallas_call | solution.py:262
  52.1 10.0 %all-to-all-start.1 = ((bf16[8,88,128]{2,1,0:T(8,128)(2,1)}), bf16[8,88,128]{2,1,0:T(8,128)(2,1)S(1)}, u32[]{:S(2)}, u32[]{:S(2)}) async-start(bf16[8,88,128]{2,1,0:T(8,128)(2,1)} %block_total.1), calls=%async_computation.1 | async-start | bytes 360448 | tf_op jit(solution)/shard_map/all_to_all | solution.py:269
  62.1 0.0 copy-done.6
  62.2 0.0 copy-done
  62.2 0.0 copy-done.2
  62.2 0.0 copy-done.3
  62.2 0.0 copy-done.4
  62.2 0.0 copy-done.5
  62.2 4.9 %inner_outputs.1 = (f32[2,128,5120]{2,1,0:T(8,128)}, f32[8,128]{1,0:T(8,128)S(1)}) custom-call(bf16[128,5120]{1,0:T(8,128)(2,1)S(1)} %copy-done, bf16[80,128]{1,0:T(8,128)(2,1)S(1)} %bitcast.8, bf16[80,128]{1,0:T(8,128)(2,1)S(1)} %bitcast.10, bf16[128,128]{1,0:T(8,128)(2,1)S(1)} %copy-done.2, bf16[128,128]{1,0:T(8,128)(2,1)S(1)} %copy-done.3, ...), custom_call_target="tpu_custom_call" | custom-call | bytes 12000000 | tf_op jit(solution)/shard_map/inner_outputs/pallas_call | solution.py:271
  67.1 4.0 %all-to-all-done.1.u_ref = bf16[8,88,128]{2,1,0:T(8,128)(2,1)S(1)} async-done(((bf16[8,88,128]{2,1,0:T(8,128)(2,1)}), bf16[8,88,128]{2,1,0:T(8,128)(2,1)S(1)}, u32[]{:S(2)}, u32[]{:S(2)}) %all-to-all-start.1) | async-done | bytes 180256 | tf_op jit(solution)/shard_map/all_to_all | solution.py:269
  71.1 0.0 copy-start.1
  71.1 0.8 entering_states.1
  71.9 41.7 %all_to_all.16 = bf16[64,80,128]{2,1,0:T(8,128)(2,1)S(1)} all-to-all(bf16[64,80,128]{2,1,0:T(8,128)(2,1)S(1)} %entering_states.1), channel_id=1, replica_groups={{0,1,2,3,4,5,6,7,8,9,10,11,12,13,14,15,16,17,18,19,20,21,22,23,24,25,26..., dimensions={0} | all-to-all | bytes 2621440 | tf_op jit(solution)/shard_map/all_to_all | solution.py:294
  113.6 0.0 copy-done.1
  113.6 1.3 %outputs.1 = bf16[128,5120]{1,0:T(8,128)(2,1)} custom-call(f32[2,128,5120]{2,1,0:T(8,128)S(1)} %copy-done.1, bf16[128,128]{1,0:T(8,128)(2,1)S(1)} %copy-done.3, bf16[8,8,80,128]{3,2,1,0:T(8,128)(2,1)S(1)} %bitcast.6), custom_call_target="tpu_custom_call" | custom-call | tf_op jit(solution)/shard_map/outputs/pallas_call | solution.py:295
  (2 shorter events, 0.0 us)
Async XLA Ops:
  50.6 11.6 %copy-start.6 = (f32[80]{0:T(128)S(1)}, f32[80]{0:T(128)}, u32[]{:S(2)}) copy-start(f32[80]{0:T(128)} %param.11) | copy-start | bytes 964
  50.6 11.6 %copy-start = (bf16[128,5120]{1,0:T(8,128)(2,1)S(1)}, bf16[128,5120]{1,0:T(8,128)(2,1)}, u32[]{:S(2)}) copy-start(bf16[128,5120]{1,0:T(8,128)(2,1)} %x_ref.3) | copy-start | bytes 3932164
  50.6 11.6 %copy-start.2 = (bf16[128,128]{1,0:T(8,128)(2,1)S(1)}, bf16[128,128]{1,0:T(8,128)(2,1)}, u32[]{:S(2)}) copy-start(bf16[128,128]{1,0:T(8,128)(2,1)} %in_hbm.1) | copy-start | bytes 98308
  50.6 11.6 %copy-start.3 = (bf16[128,128]{1,0:T(8,128)(2,1)S(1)}, bf16[128,128]{1,0:T(8,128)(2,1)}, u32[]{:S(2)}) copy-start(bf16[128,128]{1,0:T(8,128)(2,1)} %map_ref.3) | copy-start | bytes 98308
  50.6 11.6 %copy-start.4 = (bf16[128,80]{0,1:T(8,128)(2,1)S(1)}, bf16[128,80]{0,1:T(8,128)(2,1)}, u32[]{:S(2)}) copy-start(bf16[128,80]{0,1:T(8,128)(2,1)} %param.7) | copy-start | bytes 61444
  50.6 11.6 %copy-start.5 = (bf16[128,80]{0,1:T(8,128)(2,1)S(1)}, bf16[128,80]{0,1:T(8,128)(2,1)}, u32[]{:S(2)}) copy-start(bf16[128,80]{0,1:T(8,128)(2,1)} %param.8) | copy-start | bytes 61444
  52.1 19.0 %all-to-all-start.1 = ((bf16[8,88,128]{2,1,0:T(8,128)(2,1)}), bf16[8,88,128]{2,1,0:T(8,128)(2,1)S(1)}, u32[]{:S(2)}, u32[]{:S(2)}) async-start(bf16[8,88,128]{2,1,0:T(8,128)(2,1)} %block_total.1), calls=%async_computation.1 | async-start | bytes 360448 | tf_op jit(solution)/shard_map/all_to_all | solution.py:269
  71.1 42.5 %copy-start.1 = (f32[2,128,5120]{2,1,0:T(8,128)S(1)}, f32[2,128,5120]{2,1,0:T(8,128)}, u32[]{:S(2)}) copy-start(f32[2,128,5120]{2,1,0:T(8,128)} %get-tuple-element.7.part_ref) | copy-start | bytes 15728644
